TPU v7x, 32 devices: a whole 2x2x4 slice. The times are simulated.
32 devices in a mesh: dp: 4 (over z), fsdp: 8 (over y, x, core).
Axes of the slice: x: 2, y: 2, z: 4, core: 2. Of those that a mesh axis runs over, the one named last changes fastest.
Arguments:
- word_table: float32 [30720, 128], P(('dp', 'fsdp')), may hold values from -0.875 to 0.875
- position_table: float32 [512, 128], P(('dp', 'fsdp')), may hold values from -0.875 to 0.875
- head_weights: float32 [768, 1024], P(None, ('dp', 'fsdp'))
- decoder_bias: float32 [30720], P(('dp', 'fsdp')), may hold values from -1.25 to 1.25
- layer_wide: float32 [768, 6144], P(None, ('dp', 'fsdp'))
- layer_tall: float32 [3072, 768], P(('dp', 'fsdp')), may hold values from -0.109375 to 0.109375
- vectors: float32 [13184], replicated
- word_first: float32 [30720, 128], P(('dp', 'fsdp')), may hold values from -4.7683716e-07 to 4.7683716e-07
- word_second: float32 [30720, 128], P(('dp', 'fsdp')), may hold values from 5.2494893e-16 to 2.0997957e-15
- position_first: float32 [512, 128], P(('dp', 'fsdp')), may hold values from -4.7683716e-07 to 4.7683716e-07
- position_second: float32 [512, 128], P(('dp', 'fsdp')), may hold values from 5.2494893e-16 to 2.0997957e-15
- head_first: float32 [768, 1024], P(None, ('dp', 'fsdp')), may hold values from -9.536743e-07 to 9.536743e-07
- head_second: float32 [768, 1024], P(None, ('dp', 'fsdp')), may hold values from 2.0997957e-15 to 8.399183e-15
- decoder_first: float32 [30720], P(('dp', 'fsdp')), may hold values from -4.7683716e-07 to 4.7683716e-07
- decoder_second: float32 [30720], P(('dp', 'fsdp')), may hold values from 5.2494893e-16 to 2.0997957e-15
- wide_first: float32 [768, 6144], P(None, ('dp', 'fsdp')), may hold values from -9.536743e-07 to 9.536743e-07
- wide_second: float32 [768, 6144], P(None, ('dp', 'fsdp')), may hold values from 2.0997957e-15 to 8.399183e-15
- tall_first: float32 [3072, 768], P(('dp', 'fsdp')), may hold values from -9.536743e-07 to 9.536743e-07
- tall_second: float32 [3072, 768], P(('dp', 'fsdp')), may hold values from 2.0997957e-15 to 8.399183e-15
- vector_first: float32 [13184], replicated, may hold values from -3.8146973e-06 to 3.8146973e-06
- vector_second: float32 [13184], replicated, may hold values from 3.3596732e-14 to 1.3438693e-13
- token_ids: int32 [8192], P(('dp', 'fsdp')), may hold values from 0 to 30719
- seq_lengths: int32 [64], P(('dp', 'fsdp')), may hold values from 0 to 256, as said below
- mlm_rows: int32 [1280], P(('dp', 'fsdp')), may hold values from 0 to 255, as said below
- mlm_labels: int32 [1280], P(('dp', 'fsdp')), may hold values from -1 to 30719, as said below
- sop_labels: int32 [64], P(('dp', 'fsdp')), may hold values from 0 to 1
Outputs:
- word_new: float32 [30720, 128], P(('dp', 'fsdp'))
- word_first_new: float32 [30720, 128], P(('dp', 'fsdp'))
- word_second_new: float32 [30720, 128], P(('dp', 'fsdp'))
- position_new: float32 [512, 128], P(('dp', 'fsdp'))
- position_first_new: float32 [512, 128], P(('dp', 'fsdp'))
- position_second_new: float32 [512, 128], P(('dp', 'fsdp'))
- head_new: float32 [768, 1024], P(None, ('dp', 'fsdp'))
- head_first_new: float32 [768, 1024], P(None, ('dp', 'fsdp'))
- head_second_new: float32 [768, 1024], P(None, ('dp', 'fsdp'))
- decoder_new: float32 [30720], P(('dp', 'fsdp'))
- decoder_first_new: float32 [30720], P(('dp', 'fsdp'))
- decoder_second_new: float32 [30720], P(('dp', 'fsdp'))
- wide_new: float32 [768, 6144], P(None, ('dp', 'fsdp'))
- wide_first_new: float32 [768, 6144], P(None, ('dp', 'fsdp'))
- wide_second_new: float32 [768, 6144], P(None, ('dp', 'fsdp'))
- tall_new: float32 [3072, 768], P(('dp', 'fsdp'))
- tall_first_new: float32 [3072, 768], P(('dp', 'fsdp'))
- tall_second_new: float32 [3072, 768], P(('dp', 'fsdp'))
- vectors_new: float32 [13184], replicated
- vector_first_new: float32 [13184], replicated
- vector_second_new: float32 [13184], replicated
- mlm_sum: float32 [], replicated
- mlm_count: float32 [], replicated
- sop_sum: float32 [], replicated
- sop_count: float32 [], replicated
- grad_norm: float32 [], replicated
Inputs may be any that keep to these rules, and one draw needn't show every extreme that they name: `seq_lengths`: per device either one sequence of length l0 in (128, 256] with l1 = 0, or two sequences of lengths in [64, 128], the second starting at row 128. Some device holds a sequence of 256. `mlm_rows`: each slot names a live row of its own device's block. `mlm_labels`: -1 marks an unused slot; the others are word ids. Used slots come first on each device.
All inputs are finite; a program needn't handle non-finite values.
Results may differ from a plain program's by a relative error of at most 0.0085.
The roundings to bfloat16 on the way count: a program that leaves them out, or rounds other values in their place, can miss the bound.
Values may be sent and summed in bfloat16 or wider, within the bound.
A program may use at most 192 MiB of HBM per device.

v0:
```python
import jax
import jax.numpy as jnp
from jax import lax
from jax.sharding import PartitionSpec as P

D = 768
HEADS = 12
HEAD_DIM = 64
FF = 3072
E = 128
LAYERS = 4
STEP = 10
BUCKET = 128


PRECISE = lax.Precision.HIGHEST
EPSILON = 1e-06
LEARN_RATE = 0.1
SMALL_RATE = 0.5
BETA_ONE = 0.9
BETA_TWO = 0.999
ADAM_EPSILON = 1e-08
WEIGHT_DECAY = 0.01
CLIP_NORM = 0.005
NORM_EPSILON = 1e-06
MASKED = -1e30


def layout():
    return [
        ("proj_b", D),
        ("q_b", D),
        ("v_b", D),
        ("o_b", D),
        ("ln1_g", D),
        ("ln1_b", D),
        ("ffo_b", D),
        ("ln2_g", D),
        ("ln2_b", D),
        ("pool_b", D),
        ("cls", 2 * D),
        ("ff_b", FF),
        ("emb_g", E),
        ("emb_b", E),
        ("mlm_b", E),
        ("mlm_g", E),
        ("mlm_lb", E),
        ("types", 2 * E),
    ]


def split_vectors(vectors):
    pieces = {}
    offset = 0
    for member, length in layout():
        pieces[member] = vectors[offset : offset + length]
        offset += length
    return pieces


def join_vectors(gradients):
    return jnp.concatenate([gradients[member] for member, length in layout()])


def layer_norm(x, factor, offset):
    centre = x - jnp.mean(x, -1, keepdims=True)
    spread = jnp.mean(centre * centre, -1, keepdims=True)
    return centre * lax.rsqrt(spread + EPSILON) * factor + offset


def gelu_tanh(x):
    return jax.nn.gelu(x, approximate=True)


def to_half(x):
    return x.astype(jnp.bfloat16)


def product(a, b):
    return jnp.dot(a, b, preferred_element_type=jnp.float32)


def times_transpose(a, b):
    return lax.dot_general(a, b, (((1,), (1,)), ((), ())), preferred_element_type=jnp.float32)


def transpose_times(a, b):
    return lax.dot_general(a, b, (((0,), (0,)), ((), ())), preferred_element_type=jnp.float32)


def column_sum(x):
    return jnp.sum(x.astype(jnp.float32), 0)


def row_layout(lengths):
    row_index = jnp.arange(2 * BUCKET, dtype=jnp.int32)
    second = (row_index >= BUCKET) & (lengths[1] > 0)
    seq_id = second.astype(jnp.int32)
    position = row_index - BUCKET * seq_id
    own_length = jnp.where(second, lengths[1], lengths[0])
    is_live = position < own_length
    token_kind = (position >= own_length // 2).astype(jnp.int32)
    allowed = (seq_id[:, None] == seq_id[None, :]) & is_live[None, :]
    return (position, token_kind, allowed)


def embed_rows(word, place, pieces, token_ids, position, token_kind):
    types = pieces["types"].reshape(2, E)
    return (
        word[token_ids].astype(jnp.float32)
        + place[position].astype(jnp.float32)
        + types[token_kind]
    )


def embed_forward(word, place, head, pieces, token_ids, position, token_kind):
    embedded = embed_rows(word, place, pieces, token_ids, position, token_kind)
    normed_half = to_half(layer_norm(embedded, pieces["emb_g"], pieces["emb_b"]))
    return times_transpose(normed_half, head[:, E + D :]) + pieces["proj_b"]


def embed_backward(upstream, word, place, head, pieces, token_ids, position, token_kind):
    embedded = embed_rows(word, place, pieces, token_ids, position, token_kind)
    normed, norm_back = jax.vjp(layer_norm, embedded, pieces["emb_g"], pieces["emb_b"])
    normed_half = to_half(normed)
    upstream_half = to_half(upstream)
    back_proj = transpose_times(upstream_half, normed_half)
    back_rows, back_factor, back_offset = norm_back(product(upstream_half, head[:, E + D :]))
    back_word = jnp.zeros((word.shape[0], E), jnp.float32).at[token_ids].add(back_rows)
    back_place = jnp.zeros((place.shape[0], E), jnp.float32).at[position].add(back_rows)
    kind_zero = jnp.sum(jnp.where(token_kind[:, None] == 0, back_rows, 0.0), 0)
    kind_one = jnp.sum(jnp.where(token_kind[:, None] == 1, back_rows, 0.0), 0)
    vectors = {
        "proj_b": column_sum(upstream_half),
        "emb_g": back_factor,
        "emb_b": back_offset,
        "types": jnp.concatenate([kind_zero, kind_one]),
    }
    return (back_word, back_place, back_proj, vectors)


def layer_forward(hidden, weights, pieces, allowed):
    wide, tall = weights
    total_rows = hidden.shape[0]
    hidden_half = to_half(hidden)
    joint_bias = jnp.concatenate([pieces["q_b"], jnp.zeros_like(pieces["q_b"]), pieces["v_b"]])
    projected = to_half(product(hidden_half, wide[:, : 3 * D]) + joint_bias)
    heads = projected.reshape(total_rows, 3, HEADS, HEAD_DIM)
    queries, key_rows, values = (heads[:, 0], heads[:, 1], heads[:, 2])
    scores = jnp.einsum(
        "qhd,khd->hqk", queries, key_rows, preferred_element_type=jnp.float32
    ) * HEAD_DIM ** (-0.5)
    scores = jnp.where(allowed[None], scores, MASKED)
    powers = jnp.exp(scores - jnp.max(scores, -1, keepdims=True))
    weighting = powers / jnp.sum(powers, -1, keepdims=True)
    weighting_half = to_half(weighting)
    mixed = jnp.einsum("hqk,khd->qhd", weighting_half, values, preferred_element_type=jnp.float32)
    mixed = to_half(mixed.reshape(total_rows, D))
    first_sum = hidden + product(mixed, wide[:, 3 * D : 4 * D]) + pieces["o_b"]
    middle = layer_norm(first_sum, pieces["ln1_g"], pieces["ln1_b"])
    middle_half = to_half(middle)
    inner = product(middle_half, wide[:, 4 * D :]) + pieces["ff_b"]
    active = to_half(gelu_tanh(inner))
    second_sum = middle + product(active, tall) + pieces["ffo_b"]
    output = layer_norm(second_sum, pieces["ln2_g"], pieces["ln2_b"])
    kept = {
        "hidden_half": hidden_half,
        "queries": queries,
        "key_rows": key_rows,
        "values": values,
        "weighting": weighting,
        "weighting_half": weighting_half,
        "mixed": mixed,
        "first_sum": first_sum,
        "middle_half": middle_half,
        "inner": inner,
        "active": active,
        "second_sum": second_sum,
    }
    return (output, kept)


def layer_backward(hidden, weights, pieces, allowed, upstream):
    wide, tall = weights
    total_rows = hidden.shape[0]
    scale_factor = HEAD_DIM ** (-0.5)
    output, kept = layer_forward(hidden, weights, pieces, allowed)
    unused_two, second_back = jax.vjp(
        layer_norm, kept["second_sum"], pieces["ln2_g"], pieces["ln2_b"]
    )
    back_second, back_gain_two, back_shift_two = second_back(upstream)
    outer_half = to_half(back_second)
    back_tall = transpose_times(kept["active"], outer_half)
    back_active = times_transpose(outer_half, tall)
    unused_act, gelu_back = jax.vjp(gelu_tanh, kept["inner"])
    inner_half = to_half(gelu_back(back_active)[0])
    back_inner_w = transpose_times(kept["middle_half"], inner_half)
    back_middle = back_second + times_transpose(inner_half, wide[:, 4 * D :])
    unused_one, first_back = jax.vjp(
        layer_norm, kept["first_sum"], pieces["ln1_g"], pieces["ln1_b"]
    )
    back_first, back_gain_one, back_shift_one = first_back(back_middle)
    branch_half = to_half(back_first)
    back_out_w = transpose_times(kept["mixed"], branch_half)
    back_mixed = to_half(times_transpose(branch_half, wide[:, 3 * D : 4 * D])).reshape(
        total_rows, HEADS, HEAD_DIM
    )
    weighting = kept["weighting"]
    back_soft = jnp.einsum(
        "qhd,khd->hqk", back_mixed, kept["values"], preferred_element_type=jnp.float32
    )
    back_scores = weighting * (back_soft - jnp.sum(weighting * back_soft, -1, keepdims=True))
    scores_half = to_half(back_scores)
    back_queries = (
        jnp.einsum(
            "hqk,khd->qhd", scores_half, kept["key_rows"], preferred_element_type=jnp.float32
        )
        * scale_factor
    )
    back_key_rows = (
        jnp.einsum("hqk,qhd->khd", scores_half, kept["queries"], preferred_element_type=jnp.float32)
        * scale_factor
    )
    back_values = jnp.einsum(
        "hqk,qhd->khd", kept["weighting_half"], back_mixed, preferred_element_type=jnp.float32
    )
    joint_half = to_half(
        jnp.stack([back_queries, back_key_rows, back_values], 1).reshape(total_rows, 3 * D)
    )
    back_joint_w = transpose_times(kept["hidden_half"], joint_half)
    back_hidden = back_first + times_transpose(joint_half, wide[:, : 3 * D])
    joint_sum = column_sum(joint_half)
    back_wide = jnp.concatenate([back_joint_w, back_out_w, back_inner_w], 1)
    vectors = {
        "q_b": joint_sum[:D],
        "v_b": joint_sum[2 * D :],
        "o_b": column_sum(branch_half),
        "ln1_g": back_gain_one,
        "ln1_b": back_shift_one,
        "ff_b": column_sum(inner_half),
        "ffo_b": column_sum(outer_half),
        "ln2_g": back_gain_two,
        "ln2_b": back_shift_two,
    }
    return (back_hidden, back_wide, back_tall, vectors)


def head_terms(
    final, word, head, decoder, pieces, mlm_rows, mlm_labels, sop_labels, lengths, scales
):
    picked = to_half(final[mlm_rows])
    dense = product(picked, head[:, :E]) + pieces["mlm_b"]
    activated, gelu_back = jax.vjp(gelu_tanh, dense)
    head_rows, norm_back = jax.vjp(layer_norm, activated, pieces["mlm_g"], pieces["mlm_lb"])
    rows_half = to_half(head_rows)
    logits = times_transpose(rows_half, word) + decoder.astype(jnp.float32)
    top = jnp.max(logits, -1, keepdims=True)
    powers = jnp.exp(logits - top)
    totals = jnp.sum(powers, -1, keepdims=True)
    log_total = jnp.log(totals[:, 0]) + top[:, 0]
    vocab_index = jnp.arange(word.shape[0], dtype=jnp.int32)
    onehot = (vocab_index[None, :] == mlm_labels[:, None]).astype(jnp.float32)
    target = jnp.sum(logits * onehot, -1)
    used = (mlm_labels >= 0).astype(jnp.float32)
    mlm_sum = jnp.sum((log_total - target) * used)
    logits_half = to_half((powers / totals - onehot) * (used * scales[0])[:, None])
    back_decoder = column_sum(logits_half)
    back_word = transpose_times(logits_half, rows_half)
    back_act, back_mlm_g, back_mlm_lb = norm_back(product(logits_half, word))
    dense_half = to_half(gelu_back(back_act)[0])
    back_mlm = transpose_times(picked, dense_half)
    back_picked = times_transpose(dense_half, head[:, :E])
    back_final = jnp.zeros_like(final).at[mlm_rows].add(back_picked)
    firsts = to_half(jnp.concatenate([final[0:1], final[BUCKET : BUCKET + 1]], 0))
    pooled = jnp.tanh(product(firsts, head[:, E : E + D]) + pieces["pool_b"])
    classifier = pieces["cls"].reshape(2, D)
    classes = jnp.dot(pooled, classifier.T, precision=PRECISE)
    class_top = jnp.max(classes, -1, keepdims=True)
    class_powers = jnp.exp(classes - class_top)
    class_totals = jnp.sum(class_powers, -1, keepdims=True)
    class_onehot = (jnp.arange(2, dtype=jnp.int32)[None, :] == sop_labels[:, None]).astype(
        jnp.float32
    )
    present = jnp.stack([jnp.ones_like(lengths[0]), (lengths[1] > 0).astype(jnp.int32)]).astype(
        jnp.float32
    )
    sop_sum = jnp.sum(
        (jnp.log(class_totals[:, 0]) + class_top[:, 0] - jnp.sum(classes * class_onehot, -1))
        * present
    )
    back_classes = (class_powers / class_totals - class_onehot) * (present * scales[1])[:, None]
    back_cls = jnp.dot(back_classes.T, pooled, precision=PRECISE).reshape(-1)
    back_pooled = jnp.dot(back_classes, classifier, precision=PRECISE)
    pre_half = to_half(back_pooled * (1.0 - pooled * pooled))
    back_pool = transpose_times(firsts, pre_half)
    back_firsts = times_transpose(pre_half, head[:, E : E + D])
    back_final = back_final.at[0].add(back_firsts[0]).at[BUCKET].add(back_firsts[1])
    vectors = {
        "mlm_b": column_sum(dense_half),
        "mlm_g": back_mlm_g,
        "mlm_lb": back_mlm_lb,
        "pool_b": column_sum(pre_half),
        "cls": back_cls,
    }
    return (back_final, back_word, back_decoder, back_mlm, back_pool, vectors, mlm_sum, sop_sum)


def adam_update(weight, gradient, first, second, rate):
    first = BETA_ONE * first + (1 - BETA_ONE) * gradient
    second = BETA_TWO * second + (1 - BETA_TWO) * gradient * gradient
    first_hat = first / (1 - BETA_ONE**STEP)
    second_hat = second / (1 - BETA_TWO**STEP)
    updated = weight - rate * (
        first_hat / (jnp.sqrt(second_hat) + ADAM_EPSILON) + WEIGHT_DECAY * weight
    )
    return (updated, first, second)


def local(
    word_table,
    position_table,
    head_weights,
    decoder_bias,
    layer_wide,
    layer_tall,
    vectors,
    word_first,
    word_second,
    position_first,
    position_second,
    head_first,
    head_second,
    decoder_first,
    decoder_second,
    wide_first,
    wide_second,
    tall_first,
    tall_second,
    vector_first,
    vector_second,
    token_ids,
    seq_lengths,
    mlm_rows,
    mlm_labels,
    sop_labels,
):
    mlm_count, sop_count = lax.psum(
        (
            jnp.sum((mlm_labels >= 0).astype(jnp.float32)),
            (1 + (seq_lengths[1] > 0).astype(jnp.int32)).astype(jnp.float32),
        ),
        ("dp", "fsdp"),
    )
    scales = jnp.stack([1.0 / mlm_count, 1.0 / sop_count])
    pieces = split_vectors(vectors)
    position, token_kind, allowed = row_layout(seq_lengths)
    word, place, head, decoder = (
        lax.all_gather(to_half(word_table), ("dp", "fsdp"), axis=0, tiled=True),
        lax.all_gather(to_half(position_table), ("dp", "fsdp"), axis=0, tiled=True),
        lax.all_gather(to_half(head_weights), ("dp", "fsdp"), axis=1, tiled=True),
        lax.all_gather(to_half(decoder_bias), ("dp", "fsdp"), axis=0, tiled=True),
    )

    def fetch_forward():
        fetched = (
            lax.all_gather(to_half(layer_wide), ("dp", "fsdp"), axis=1, tiled=True),
            lax.all_gather(to_half(layer_tall), ("dp", "fsdp"), axis=0, tiled=True),
        )
        return fetched

    def fetch_back():
        fetched = (
            lax.all_gather(to_half(layer_wide), ("dp", "fsdp"), axis=1, tiled=True),
            lax.all_gather(to_half(layer_tall), ("dp", "fsdp"), axis=0, tiled=True),
        )
        return fetched

    hidden = embed_forward(word, place, head, pieces, token_ids, position, token_kind)

    def forward_step(current, unused):
        output, kept = layer_forward(current, fetch_forward(), pieces, allowed)
        return (output, current)

    final, inputs = lax.scan(forward_step, hidden, None, length=LAYERS)
    (
        back_final,
        back_word_head,
        back_decoder,
        back_mlm,
        back_pool,
        head_vectors,
        mlm_sum,
        sop_sum,
    ) = head_terms(
        final, word, head, decoder, pieces, mlm_rows, mlm_labels, sop_labels, seq_lengths, scales
    )
    layer_names = ("q_b", "v_b", "o_b", "ln1_g", "ln1_b", "ff_b", "ffo_b", "ln2_g", "ln2_b")
    vector_zero = {member: jnp.zeros_like(pieces[member]) for member in layer_names}
    wide_shape = layer_wide.shape
    tall_shape = layer_tall.shape

    def backward_step(carry, current):
        upstream, sum_wide, sum_tall, sum_vectors = carry
        back_hidden, back_wide, back_tall, back_vectors = layer_backward(
            current, fetch_back(), pieces, allowed, upstream
        )
        back_wide, back_tall = (
            lax.psum_scatter(back_wide, ("dp", "fsdp"), scatter_dimension=1, tiled=True),
            lax.psum_scatter(back_tall, ("dp", "fsdp"), scatter_dimension=0, tiled=True),
        )
        summed = jax.tree.map(jnp.add, sum_vectors, back_vectors)
        return ((back_hidden, sum_wide + back_wide, sum_tall + back_tall, summed), None)

    start = (
        back_final,
        jnp.zeros(wide_shape, jnp.float32),
        jnp.zeros(tall_shape, jnp.float32),
        vector_zero,
    )
    finish, unused_out = lax.scan(backward_step, start, inputs, reverse=True)
    back_embed, sum_wide, sum_tall, layer_vectors = finish
    back_word_rows, back_place, back_proj, embed_vectors = embed_backward(
        back_embed, word, place, head, pieces, token_ids, position, token_kind
    )
    back_word = back_word_rows + back_word_head
    back_head = jnp.concatenate([back_mlm, back_pool, back_proj], 1)
    merged = dict(layer_vectors)
    merged.update(embed_vectors)
    merged.update(head_vectors)
    vector_grad = join_vectors(merged)
    outer = (
        lax.psum_scatter(back_word, ("dp", "fsdp"), scatter_dimension=0, tiled=True),
        lax.psum_scatter(back_place, ("dp", "fsdp"), scatter_dimension=0, tiled=True),
        lax.psum_scatter(back_head, ("dp", "fsdp"), scatter_dimension=1, tiled=True),
        lax.psum_scatter(back_decoder, ("dp", "fsdp"), scatter_dimension=0, tiled=True),
    )
    shards = tuple(outer) + (sum_wide, sum_tall)
    reduced_vectors, mlm_total, sop_total = lax.psum(
        (vector_grad, mlm_sum, sop_sum), ("dp", "fsdp")
    )
    local_squares = jnp.sum(jnp.stack([jnp.sum(s * s) for s in shards]))
    total_squares = lax.psum(local_squares, ("dp", "fsdp")) + jnp.sum(
        reduced_vectors * reduced_vectors
    )
    grad_norm = jnp.sqrt(total_squares)
    factor = jnp.minimum(1.0, CLIP_NORM / (grad_norm + NORM_EPSILON))
    word_new, word_first_new, word_second_new = adam_update(
        word_table, factor * shards[0], word_first, word_second, LEARN_RATE
    )
    position_new, position_first_new, position_second_new = adam_update(
        position_table, factor * shards[1], position_first, position_second, LEARN_RATE
    )
    head_new, head_first_new, head_second_new = adam_update(
        head_weights, factor * shards[2], head_first, head_second, LEARN_RATE
    )
    decoder_new, decoder_first_new, decoder_second_new = adam_update(
        decoder_bias, factor * shards[3], decoder_first, decoder_second, LEARN_RATE
    )
    wide_new, wide_first_new, wide_second_new = adam_update(
        layer_wide, factor * shards[4], wide_first, wide_second, LEARN_RATE
    )
    tall_new, tall_first_new, tall_second_new = adam_update(
        layer_tall, factor * shards[5], tall_first, tall_second, LEARN_RATE
    )
    vectors_new, vector_first_new, vector_second_new = adam_update(
        vectors, factor * reduced_vectors, vector_first, vector_second, SMALL_RATE
    )
    return (
        word_new,
        word_first_new,
        word_second_new,
        position_new,
        position_first_new,
        position_second_new,
        head_new,
        head_first_new,
        head_second_new,
        decoder_new,
        decoder_first_new,
        decoder_second_new,
        wide_new,
        wide_first_new,
        wide_second_new,
        tall_new,
        tall_first_new,
        tall_second_new,
        vectors_new,
        vector_first_new,
        vector_second_new,
        mlm_total,
        mlm_count,
        sop_total,
        sop_count,
        grad_norm,
    )


def solution(mesh):
    return jax.shard_map(
        local,
        mesh=mesh,
        in_specs=(
            P(("dp", "fsdp"), None),
            P(("dp", "fsdp"), None),
            P(None, ("dp", "fsdp")),
            P(("dp", "fsdp")),
            P(None, ("dp", "fsdp")),
            P(("dp", "fsdp"), None),
            P(),
            P(("dp", "fsdp"), None),
            P(("dp", "fsdp"), None),
            P(("dp", "fsdp"), None),
            P(("dp", "fsdp"), None),
            P(None, ("dp", "fsdp")),
            P(None, ("dp", "fsdp")),
            P(("dp", "fsdp")),
            P(("dp", "fsdp")),
            P(None, ("dp", "fsdp")),
            P(None, ("dp", "fsdp")),
            P(("dp", "fsdp"), None),
            P(("dp", "fsdp"), None),
            P(),
            P(),
            P(("dp", "fsdp")),
            P(("dp", "fsdp")),
            P(("dp", "fsdp")),
            P(("dp", "fsdp")),
            P(("dp", "fsdp")),
        ),
        out_specs=(
            P(("dp", "fsdp"), None),
            P(("dp", "fsdp"), None),
            P(("dp", "fsdp"), None),
            P(("dp", "fsdp"), None),
            P(("dp", "fsdp"), None),
            P(("dp", "fsdp"), None),
            P(None, ("dp", "fsdp")),
            P(None, ("dp", "fsdp")),
            P(None, ("dp", "fsdp")),
            P(("dp", "fsdp")),
            P(("dp", "fsdp")),
            P(("dp", "fsdp")),
            P(None, ("dp", "fsdp")),
            P(None, ("dp", "fsdp")),
            P(None, ("dp", "fsdp")),
            P(("dp", "fsdp"), None),
            P(("dp", "fsdp"), None),
            P(("dp", "fsdp"), None),
            P(),
            P(),
            P(),
            P(),
            P(),
            P(),
            P(),
            P(),
        ),
        check_vma=False,
    )
```

profile of v0, /device:TPU:0, one launch (start us, length us, event | category | flops | bytes accessed | tf_op | source)
XLA Modules:
  0.0 3525.6 jit_solution(1169098214806725181)
XLA Ops:
  148.8 635.3 %while.54 = (s32[]{:T(128)}, f32[256,768]{1,0:T(8,128)S(1)}, f32[4,256,768]{2,1,0:T(8,128)}, bf16[768,192]{0,1:T(8,128)(2,1)}, f32[768]{0:T(1024)S(1)}, /*index=...) while((s32[]{:T(128)}, f32[256,768]{1,0:T(8,128)S(1)}, ...), condition=%wide.region_9.10_spmd.clone, body=%wide.region_2.9_spmd.clone.sunk | while | flops 3845985536 | bytes 85791288 | solution.py:384
  151.4 83.3 %all-gather.13.cloned.1.call-done = bf16[768,6144]{0,1:T(8,128)(2,1)} async-done(((bf16[768,192]{0,1:T(8,128)(2,1)}), bf16[768,6144]{0,1:T(8,128)(2,1)}) %all-gather.13.cloned.1.call-update) | async-done | bytes 9437200 | tf_op jit(solution)/shard_map/while/body/eval_jaxpr/all_gather | solution.py:366
  310.2 83.0 %all-gather.13.cloned.1.call-done = bf16[768,6144]{0,1:T(8,128)(2,1)} async-done(((bf16[768,192]{0,1:T(8,128)(2,1)}), bf16[768,6144]{0,1:T(8,128)(2,1)}) %all-gather.13.cloned.1.call-update) | async-done | bytes 9437200 | tf_op jit(solution)/shard_map/while/body/eval_jaxpr/all_gather | solution.py:366
  401.1 58.1 %all-gather.11.cloned.1.call-done = bf16[3072,768]{1,0:T(8,128)(2,1)} async-done(((bf16[96,768]{1,0:T(8,128)(2,1)}), bf16[3072,768]{1,0:T(8,128)(2,1)}) %all-gather.11.cloned.1.call-update) | async-done | bytes 4718608 | tf_op jit(solution)/shard_map/while/body/eval_jaxpr/all_gather | solution.py:367
  469.0 83.0 %all-gather.13.cloned.1.call-done = bf16[768,6144]{0,1:T(8,128)(2,1)} async-done(((bf16[768,192]{0,1:T(8,128)(2,1)}), bf16[768,6144]{0,1:T(8,128)(2,1)}) %all-gather.13.cloned.1.call-update) | async-done | bytes 9437200 | tf_op jit(solution)/shard_map/while/body/eval_jaxpr/all_gather | solution.py:366
  559.9 58.3 %all-gather.11.cloned.1.call-done = bf16[3072,768]{1,0:T(8,128)(2,1)} async-done(((bf16[96,768]{1,0:T(8,128)(2,1)}), bf16[3072,768]{1,0:T(8,128)(2,1)}) %all-gather.11.cloned.1.call-update) | async-done | bytes 4718608 | tf_op jit(solution)/shard_map/while/body/eval_jaxpr/all_gather | solution.py:367
  627.8 83.2 %all-gather.13.cloned.1.call-done = bf16[768,6144]{0,1:T(8,128)(2,1)} async-done(((bf16[768,192]{0,1:T(8,128)(2,1)}), bf16[768,6144]{0,1:T(8,128)(2,1)}) %all-gather.13.cloned.1.call-update) | async-done | bytes 9437200 | tf_op jit(solution)/shard_map/while/body/eval_jaxpr/all_gather | solution.py:366
  857.4 2059.1 %while.55 = (s32[]{:T(128)}, f32[256,768]{1,0:T(8,128)S(1)}, f32[768,192]{1,0:T(8,128)}, f32[96,768]{1,0:T(8,128)}, f32[3072]{0:T(1024)}, /*index=5*/f32[768]{0:...) while((s32[]{:T(128)}, f32[256,768]{1,0:T(8,128)S(1)}, ...), condition=%wide.region_44.45_spmd.clone, body=%wide.region_22.44_spmd.clone.sunk | while | flops 11549339648 | bytes 444655104 | solution.py:420
  859.1 85.6 %all-gather.15.cloned.1.call-done = bf16[768,6144]{0,1:T(8,128)(2,1)} async-done(((bf16[768,192]{0,1:T(8,128)(2,1)}), bf16[768,6144]{0,1:T(8,128)(2,1)}) %all-gather.15.cloned.1.call-update) | async-done | bytes 9437200 | tf_op jit(solution)/shard_map/while/body/eval_jaxpr/all_gather | solution.py:373
  1085.8 72.7 %reduce-scatter.18.cloned.1.call-done = f32[96,768]{1,0:T(8,128)} async-done(((f32[3072,768]{1,0:T(8,128)}), f32[96,768]{1,0:T(8,128)}) %reduce-scatter.18.cloned.1.call-update) | async-done | bytes 294928 | tf_op jit(solution)/shard_map/while/body/eval_jaxpr/reduce_scatter | solution.py:409
  1160.2 210.6 %reduce-scatter.16.cloned.1.call-done = f32[192,768]{1,0:T(8,128)} async-done(((f32[6144,768]{1,0:T(8,128)}), f32[192,768]{1,0:T(8,128)}) %reduce-scatter.16.cloned.1.call-update) | async-done | bytes 589840 | tf_op jit(solution)/shard_map/while
  1374.8 84.0 %all-gather.15.cloned.1.call-done = bf16[768,6144]{0,1:T(8,128)(2,1)} async-done(((bf16[768,192]{0,1:T(8,128)(2,1)}), bf16[768,6144]{0,1:T(8,128)(2,1)}) %all-gather.15.cloned.1.call-update) | async-done | bytes 9437200 | tf_op jit(solution)/shard_map/while/body/eval_jaxpr/all_gather | solution.py:373
  1600.5 72.0 %reduce-scatter.18.cloned.1.call-done = f32[96,768]{1,0:T(8,128)} async-done(((f32[3072,768]{1,0:T(8,128)}), f32[96,768]{1,0:T(8,128)}) %reduce-scatter.18.cloned.1.call-update) | async-done | bytes 294928 | tf_op jit(solution)/shard_map/while/body/eval_jaxpr/reduce_scatter | solution.py:409
  1674.3 210.5 %reduce-scatter.16.cloned.1.call-done = f32[192,768]{1,0:T(8,128)} async-done(((f32[6144,768]{1,0:T(8,128)}), f32[192,768]{1,0:T(8,128)}) %reduce-scatter.16.cloned.1.call-update) | async-done | bytes 589840 | tf_op jit(solution)/shard_map/while
  1888.9 84.2 %all-gather.15.cloned.1.call-done = bf16[768,6144]{0,1:T(8,128)(2,1)} async-done(((bf16[768,192]{0,1:T(8,128)(2,1)}), bf16[768,6144]{0,1:T(8,128)(2,1)}) %all-gather.15.cloned.1.call-update) | async-done | bytes 9437200 | tf_op jit(solution)/shard_map/while/body/eval_jaxpr/all_gather | solution.py:373
  2114.8 72.2 %reduce-scatter.18.cloned.1.call-done = f32[96,768]{1,0:T(8,128)} async-done(((f32[3072,768]{1,0:T(8,128)}), f32[96,768]{1,0:T(8,128)}) %reduce-scatter.18.cloned.1.call-update) | async-done | bytes 294928 | tf_op jit(solution)/shard_map/while/body/eval_jaxpr/reduce_scatter | solution.py:409
  2188.7 210.5 %reduce-scatter.16.cloned.1.call-done = f32[192,768]{1,0:T(8,128)} async-done(((f32[6144,768]{1,0:T(8,128)}), f32[192,768]{1,0:T(8,128)}) %reduce-scatter.16.cloned.1.call-update) | async-done | bytes 589840 | tf_op jit(solution)/shard_map/while
  2403.4 84.2 %all-gather.15.cloned.1.call-done = bf16[768,6144]{0,1:T(8,128)(2,1)} async-done(((bf16[768,192]{0,1:T(8,128)(2,1)}), bf16[768,6144]{0,1:T(8,128)(2,1)}) %all-gather.15.cloned.1.call-update) | async-done | bytes 9437200 | tf_op jit(solution)/shard_map/while/body/eval_jaxpr/all_gather | solution.py:373
  2629.3 72.2 %reduce-scatter.18.cloned.1.call-done = f32[96,768]{1,0:T(8,128)} async-done(((f32[3072,768]{1,0:T(8,128)}), f32[96,768]{1,0:T(8,128)}) %reduce-scatter.18.cloned.1.call-update) | async-done | bytes 294928 | tf_op jit(solution)/shard_map/while/body/eval_jaxpr/reduce_scatter | solution.py:409
  2703.3 210.4 %reduce-scatter.16.cloned.1.call-done = f32[192,768]{1,0:T(8,128)} async-done(((f32[6144,768]{1,0:T(8,128)}), f32[192,768]{1,0:T(8,128)}) %reduce-scatter.16.cloned.1.call-update) | async-done | bytes 589840 | tf_op jit(solution)/shard_map/while
  2953.2 90.2 %all-reduce.6.cloned.1.call-done = f32[30720]{0:T(1024)} async-done(((f32[30720]{0:T(1024)}), f32[30720]{0:T(1024)}) %all-reduce.6.cloned.1.call-update) | async-done | bytes 122896
  3044.7 135.5 %reduce-scatter.12.cloned.1.call-done = f32[16,128]{1,0:T(8,128)} async-done(((f32[512,128]{1,0:T(8,128)}), f32[16,128]{1,0:T(8,128)}) %reduce-scatter.12.cloned.1.call-update) | async-done | bytes 8208 | tf_op jit(solution)/shard_map/reduce_scatter | solution.py:433
  3181.5 102.5 %reduce-scatter.14.cloned.1.call-done = f32[768,32]{0,1:T(8,128)} async-done(((f32[768,1024]{0,1:T(8,128)}), f32[768,32]{0,1:T(8,128)}) %reduce-scatter.14.cloned.1.call-update) | async-done | bytes 98320 | tf_op jit(solution)/shard_map/reduce_scatter | solution.py:434
  3285.5 174.9 %reduce-scatter.10.cloned.1.call-done = f32[960,128]{1,0:T(8,128)} async-done(((f32[30720,128]{1,0:T(8,128)}), f32[960,128]{1,0:T(8,128)}) %reduce-scatter.10.cloned.1.call-update) | async-done | bytes 491536 | tf_op jit(solution)/shard_map/reduce_scatter | solution.py:432
  (1153 shorter events, 1076.0 us)
Async XLA Ops:
  7.2 106.1 %all-gather.7.cloned.1.call-start = ((), (), s32[]{:S(2)}) async-start(), calls=%async_computation.5 | async-start | bytes 8110080 | tf_op jit(solution)/shard_map/all_gather | solution.py:358
  9.1 138.4 %all-gather.9.cloned.1.call-start = ((), (), s32[]{:S(2)}) async-start(), calls=%async_computation.6 | async-start | bytes 1622016 | tf_op jit(solution)/shard_map/all_gather | solution.py:360
  149.7 151.0 %all-gather.11.cloned.1.call-start = ((), (), s32[]{:S(2)}) async-start(), calls=%async_computation.11 | async-start | bytes 4866048 | tf_op jit(solution)/shard_map/while/body/eval_jaxpr/all_gather | solution.py:367
  308.5 150.7 %all-gather.11.cloned.1.call-start = ((), (), s32[]{:S(2)}) async-start(), calls=%async_computation.11 | async-start | bytes 4866048 | tf_op jit(solution)/shard_map/while/body/eval_jaxpr/all_gather | solution.py:367
  467.1 151.0 %all-gather.11.cloned.1.call-start = ((), (), s32[]{:S(2)}) async-start(), calls=%async_computation.11 | async-start | bytes 4866048 | tf_op jit(solution)/shard_map/while/body/eval_jaxpr/all_gather | solution.py:367
  626.1 150.9 %all-gather.11.cloned.1.call-start = ((), (), s32[]{:S(2)}) async-start(), calls=%async_computation.11 | async-start | bytes 4866048 | tf_op jit(solution)/shard_map/while/body/eval_jaxpr/all_gather | solution.py:367
  857.6 87.1 %all-gather.15.cloned.1.call-start = ((), (), s32[]{:S(2)}) async-start(), calls=%async_computation.13 | async-start | bytes 9732096 | tf_op jit(solution)/shard_map/while/body/eval_jaxpr/all_gather | solution.py:373
  858.3 152.4 %all-gather.17.cloned.1.call-start = ((), (), s32[]{:S(2)}) async-start(), calls=%async_computation.14 | async-start | bytes 4866048 | tf_op jit(solution)/shard_map/while/body/eval_jaxpr/all_gather | solution.py:374
  858.9 299.6 %reduce-scatter.18.cloned.1.call-start = ((), (), s32[]{:S(2)}) async-start(), calls=%async_computation.16 | async-start | bytes 9732096 | tf_op jit(solution)/shard_map/while/body/eval_jaxpr/reduce_scatter | solution.py:409
  1024.2 346.6 %reduce-scatter.16.cloned.1.call-start = ((), (), s32[]{:S(2)}) async-start(), calls=%async_computation.15 | async-start | bytes 19464192 | tf_op jit(solution)/shard_map/while
  1374.0 150.8 %all-gather.17.cloned.1.call-start = ((), (), s32[]{:S(2)}) async-start(), calls=%async_computation.14 | async-start | bytes 4866048 | tf_op jit(solution)/shard_map/while/body/eval_jaxpr/all_gather | solution.py:374
  1374.5 297.9 %reduce-scatter.18.cloned.1.call-start = ((), (), s32[]{:S(2)}) async-start(), calls=%async_computation.16 | async-start | bytes 9732096 | tf_op jit(solution)/shard_map/while/body/eval_jaxpr/reduce_scatter | solution.py:409
  1538.2 346.6 %reduce-scatter.16.cloned.1.call-start = ((), (), s32[]{:S(2)}) async-start(), calls=%async_computation.15 | async-start | bytes 19464192 | tf_op jit(solution)/shard_map/while
  1888.1 151.0 %all-gather.17.cloned.1.call-start = ((), (), s32[]{:S(2)}) async-start(), calls=%async_computation.14 | async-start | bytes 4866048 | tf_op jit(solution)/shard_map/while/body/eval_jaxpr/all_gather | solution.py:374
  1888.7 298.3 %reduce-scatter.18.cloned.1.call-start = ((), (), s32[]{:S(2)}) async-start(), calls=%async_computation.16 | async-start | bytes 9732096 | tf_op jit(solution)/shard_map/while/body/eval_jaxpr/reduce_scatter | solution.py:409
  2052.5 346.8 %reduce-scatter.16.cloned.1.call-start = ((), (), s32[]{:S(2)}) async-start(), calls=%async_computation.15 | async-start | bytes 19464192 | tf_op jit(solution)/shard_map/while
  2401.9 85.7 %all-gather.15.cloned.1.call-start = ((), (), s32[]{:S(2)}) async-start(), calls=%async_computation.13 | async-start | bytes 9732096 | tf_op jit(solution)/shard_map/while/body/eval_jaxpr/all_gather | solution.py:373
  2402.6 151.0 %all-gather.17.cloned.1.call-start = ((), (), s32[]{:S(2)}) async-start(), calls=%async_computation.14 | async-start | bytes 4866048 | tf_op jit(solution)/shard_map/while/body/eval_jaxpr/all_gather | solution.py:374
  2403.2 298.3 %reduce-scatter.18.cloned.1.call-start = ((), (), s32[]{:S(2)}) async-start(), calls=%async_computation.16 | async-start | bytes 9732096 | tf_op jit(solution)/shard_map/while/body/eval_jaxpr/reduce_scatter | solution.py:409
  2567.0 346.7 %reduce-scatter.16.cloned.1.call-start = ((), (), s32[]{:S(2)}) async-start(), calls=%async_computation.15 | async-start | bytes 19464192 | tf_op jit(solution)/shard_map/while
  2916.5 126.9 %all-reduce.6.cloned.1.call-start = ((), (), s32[]{:S(2)}) async-start(), calls=%async_computation.10 | async-start | bytes 245760
  2917.1 263.1 %reduce-scatter.12.cloned.1.call-start = ((), (), s32[]{:S(2)}) async-start(), calls=%async_computation.8 | async-start | bytes 270336 | tf_op jit(solution)/shard_map/reduce_scatter | solution.py:433
  2924.0 360.0 %reduce-scatter.14.cloned.1.call-start = ((), (), s32[]{:S(2)}) async-start(), calls=%async_computation.9 | async-start | bytes 3244032 | tf_op jit(solution)/shard_map/reduce_scatter | solution.py:434
  2926.8 533.7 %reduce-scatter.10.cloned.1.call-start = ((), (), s32[]{:S(2)}) async-start(), calls=%async_computation.7 | async-start | bytes 16220160 | tf_op jit(solution)/shard_map/reduce_scatter | solution.py:432
  (335 other events, 18971.4 us)
Sparse Core Ops, SparseCore 0:
  11.5 78.8 all-gather.6
  153.7 80.9 all-gather.12
  312.3 80.8 all-gather.12
  471.1 80.8 all-gather.12
  555.9 62.2 all-gather.10
  630.1 80.8 all-gather.12
  714.7 62.2 all-gather.10
  862.3 82.3 all-gather.14
  1024.3 134.1 reduce-scatter.17
  1164.7 205.9 reduce-scatter.15
  1377.8 80.9 all-gather.14
  1538.3 134.1 reduce-scatter.17
  1678.7 205.9 reduce-scatter.15
  1892.1 80.9 all-gather.14
  1976.8 62.2 all-gather.16
  2052.6 134.3 reduce-scatter.17
  2193.4 205.8 reduce-scatter.15
  2406.6 80.9 all-gather.14
  2567.2 134.3 reduce-scatter.17
  2707.8 205.8 reduce-scatter.15
  2923.2 120.1 all-reduce.5
  3046.2 133.9 reduce-scatter.11
  3186.5 97.4 reduce-scatter.13
  3290.9 169.4 reduce-scatter.9
  (6 shorter events, 364.4 us)
where the time goes:
time: 3530 us
  waiting for transfers between devices  2780 us (79%)
  matrix products  274 us (8%)
  blocking collectives  164 us (5%)
  local copies, waits for them, and re-layouts  142 us (4%)
  other arithmetic  135 us (4%)
    while x28, waiting for transfers between devices  852 us
    all_gather x4, waiting for transfers between devices, fetch_back(): lax.all_gather(to_half(layer_wide), ('dp', 'fsdp'), axis=1, tiled=True)  338 us
    all_gather x4, waiting for transfers between devices, fetch_forward(): lax.all_gather(to_half(layer_wide), ('dp', 'fsdp'), axis=1, tiled=True)  332 us
    reduce_scatter x4, waiting for transfers between devices, backward_step(): lax.psum_scatter(back_tall, ('dp', 'fsdp'), scatter_dimension=0, tiled=True)  289 us
    all_gather x4, waiting for transfers between devices, fetch_forward(): lax.all_gather(to_half(layer_tall), ('dp', 'fsdp'), axis=0, tiled=True)  233 us
    all_gather x4, waiting for transfers between devices, fetch_back(): lax.all_gather(to_half(layer_tall), ('dp', 'fsdp'), axis=0, tiled=True)  204 us
    reduce_scatter x1, waiting for transfers between devices, local(): lax.psum_scatter(back_word, ('dp', 'fsdp'), scatter_dimension=0, tiled=True)  175 us
    reduce_scatter x1, waiting for transfers between devices, local(): lax.psum_scatter(back_place, ('dp', 'fsdp'), scatter_dimension=0, tiled=T...  135 us
  transfers between devices with their start and end apart: 30, of which 29 were waited for; matrix products, arithmetic and copies ran while one was open for 11% of the time, Pallas kernels for 0%

commit v1 on v0

v1 whole, which is shorter than its diff:
```python
import jax
import jax.numpy as jnp
from jax import lax
from jax.sharding import PartitionSpec as P

D = 768
HEADS = 12
HEAD_DIM = 64
FF = 3072
E = 128
LAYERS = 4
STEP = 10
BUCKET = 128
ROWS = 2 * BUCKET

PRECISE = lax.Precision.HIGHEST
EPSILON = 1e-06
LEARN_RATE = 0.1
SMALL_RATE = 0.5
BETA_ONE = 0.9
BETA_TWO = 0.999
ADAM_EPSILON = 1e-08
WEIGHT_DECAY = 0.01
CLIP_NORM = 0.005
NORM_EPSILON = 1e-06
MASKED = -1e30
SCALE = HEAD_DIM ** (-0.5)
AXES = ("dp", "fsdp")


def layout():
    return [
        ("proj_b", D),
        ("q_b", D),
        ("v_b", D),
        ("o_b", D),
        ("ln1_g", D),
        ("ln1_b", D),
        ("ffo_b", D),
        ("ln2_g", D),
        ("ln2_b", D),
        ("pool_b", D),
        ("cls", 2 * D),
        ("ff_b", FF),
        ("emb_g", E),
        ("emb_b", E),
        ("mlm_b", E),
        ("mlm_g", E),
        ("mlm_lb", E),
        ("types", 2 * E),
    ]


def split_vectors(vectors):
    pieces = {}
    offset = 0
    for member, length in layout():
        pieces[member] = vectors[offset : offset + length]
        offset += length
    return pieces


def join_vectors(gradients):
    return jnp.concatenate([gradients[member].reshape(-1) for member, length in layout()])


def to_half(x):
    return x.astype(jnp.bfloat16)


def product(a, b):
    return jnp.dot(a, b, preferred_element_type=jnp.float32)


def times_transpose(a, b):
    return lax.dot_general(a, b, (((1,), (1,)), ((), ())), preferred_element_type=jnp.float32)


def transpose_times(a, b):
    return lax.dot_general(a, b, (((0,), (0,)), ((), ())), preferred_element_type=jnp.float32)


def column_sum(x):
    return jnp.sum(x.astype(jnp.float32), 0)


def norm_forward(x):
    centre = x - jnp.mean(x, -1, keepdims=True)
    inverse = lax.rsqrt(jnp.mean(centre * centre, -1, keepdims=True) + EPSILON)
    return centre * inverse, inverse


def norm_backward(upstream, factor, hat, inverse):
    scaled = upstream * factor
    return inverse * (
        scaled
        - jnp.mean(scaled, -1, keepdims=True)
        - hat * jnp.mean(scaled * hat, -1, keepdims=True)
    )


GELU_A = 0.7978845608028654
GELU_B = 0.044715


def gelu_tanh(x):
    return 0.5 * x * (1.0 + jnp.tanh(GELU_A * (x + GELU_B * x * x * x)))


def gelu_slope(x):
    bend = jnp.tanh(GELU_A * (x + GELU_B * x * x * x))
    return 0.5 * (1.0 + bend) + 0.5 * x * (1.0 - bend * bend) * GELU_A * (
        1.0 + 3.0 * GELU_B * x * x
    )


def row_layout(lengths):
    row_index = jnp.arange(ROWS, dtype=jnp.int32)
    second = (row_index >= BUCKET) & (lengths[1] > 0)
    seq_id = second.astype(jnp.int32)
    position = row_index - BUCKET * seq_id
    own_length = jnp.where(second, lengths[1], lengths[0])
    is_live = position < own_length
    token_kind = (position >= own_length // 2).astype(jnp.int32)
    allowed = (seq_id[:, None] == seq_id[None, :]) & is_live[None, :]
    return (token_kind, allowed)


def gather_rows(shards):
    return [lax.all_gather(s, AXES, axis=0, tiled=True) for s in shards]


def scatter_rows(partials):
    return [lax.psum_scatter(s, AXES, scatter_dimension=0, tiled=True) for s in partials]


def layer_forward(hidden, wide, tall, pieces, allowed):
    hidden_half = to_half(hidden)
    joint_bias = jnp.concatenate([pieces["q_b"], jnp.zeros_like(pieces["q_b"]), pieces["v_b"]])
    projected = to_half(times_transpose(hidden_half, wide[: 3 * D]) + joint_bias)
    heads = projected.reshape(ROWS, 3, HEADS, HEAD_DIM)
    queries, key_rows, values = (heads[:, 0], heads[:, 1], heads[:, 2])
    scores = (
        jnp.einsum("qhd,khd->hqk", queries, key_rows, preferred_element_type=jnp.float32) * SCALE
    )
    scores = jnp.where(allowed[None], scores, MASKED)
    powers = jnp.exp(scores - jnp.max(scores, -1, keepdims=True))
    weighting = powers / jnp.sum(powers, -1, keepdims=True)
    mixed = jnp.einsum(
        "hqk,khd->qhd", to_half(weighting), values, preferred_element_type=jnp.float32
    )
    mixed = to_half(mixed.reshape(ROWS, D))
    first_sum = hidden + times_transpose(mixed, wide[3 * D : 4 * D]) + pieces["o_b"]
    hat_one, inverse_one = norm_forward(first_sum)
    middle = hat_one * pieces["ln1_g"] + pieces["ln1_b"]
    middle_half = to_half(middle)
    inner = times_transpose(middle_half, wide[4 * D :]) + pieces["ff_b"]
    active = to_half(gelu_tanh(inner))
    second_sum = middle + product(active, tall) + pieces["ffo_b"]
    hat_two, inverse_two = norm_forward(second_sum)
    output = hat_two * pieces["ln2_g"] + pieces["ln2_b"]
    kept = {
        "hidden_half": hidden_half,
        "projected": projected,
        "weighting": weighting,
        "mixed": mixed,
        "hat_one": hat_one,
        "inverse_one": inverse_one,
        "middle_half": middle_half,
        "inner": inner,
        "active": active,
        "hat_two": hat_two,
        "inverse_two": inverse_two,
    }
    return (output, kept)


def layer_backward(upstream, kept, wide, tall, pieces):
    gain_two = jnp.sum(upstream * kept["hat_two"], 0)
    shift_two = jnp.sum(upstream, 0)
    back_second = norm_backward(upstream, pieces["ln2_g"], kept["hat_two"], kept["inverse_two"])
    outer_half = to_half(back_second)
    inner_half = to_half(times_transpose(outer_half, tall) * gelu_slope(kept["inner"]))
    back_middle = back_second + product(inner_half, wide[4 * D :])
    gain_one = jnp.sum(back_middle * kept["hat_one"], 0)
    shift_one = jnp.sum(back_middle, 0)
    back_first = norm_backward(back_middle, pieces["ln1_g"], kept["hat_one"], kept["inverse_one"])
    branch_half = to_half(back_first)
    back_mixed = to_half(product(branch_half, wide[3 * D : 4 * D])).reshape(ROWS, HEADS, HEAD_DIM)
    heads = kept["projected"].reshape(ROWS, 3, HEADS, HEAD_DIM)
    queries, key_rows, values = (heads[:, 0], heads[:, 1], heads[:, 2])
    weighting = kept["weighting"]
    back_soft = jnp.einsum("qhd,khd->hqk", back_mixed, values, preferred_element_type=jnp.float32)
    scores_half = to_half(
        weighting * (back_soft - jnp.sum(weighting * back_soft, -1, keepdims=True))
    )
    back_queries = (
        jnp.einsum("hqk,khd->qhd", scores_half, key_rows, preferred_element_type=jnp.float32)
        * SCALE
    )
    back_key_rows = (
        jnp.einsum("hqk,qhd->khd", scores_half, queries, preferred_element_type=jnp.float32) * SCALE
    )
    back_values = jnp.einsum(
        "hqk,qhd->khd", to_half(weighting), back_mixed, preferred_element_type=jnp.float32
    )
    joint_half = to_half(
        jnp.stack([back_queries, back_key_rows, back_values], 1).reshape(ROWS, 3 * D)
    )
    back_hidden = back_first + product(joint_half, wide[: 3 * D])
    out = {
        "joint_half": joint_half,
        "branch_half": branch_half,
        "inner_half": inner_half,
        "outer_half": outer_half,
        "norms": jnp.stack([gain_one, shift_one, gain_two, shift_two]),
    }
    return (back_hidden, out)


def adam_update(weight, gradient, first, second, rate):
    first = BETA_ONE * first + (1 - BETA_ONE) * gradient
    second = BETA_TWO * second + (1 - BETA_TWO) * gradient * gradient
    first_hat = first / (1 - BETA_ONE**STEP)
    second_hat = second / (1 - BETA_TWO**STEP)
    updated = weight - rate * (
        first_hat / (jnp.sqrt(second_hat) + ADAM_EPSILON) + WEIGHT_DECAY * weight
    )
    return (updated, first, second)


def local(
    word_table,
    position_table,
    head_weights,
    decoder_bias,
    layer_wide,
    layer_tall,
    vectors,
    word_first,
    word_second,
    position_first,
    position_second,
    head_first,
    head_second,
    decoder_first,
    decoder_second,
    wide_first,
    wide_second,
    tall_first,
    tall_second,
    vector_first,
    vector_second,
    token_ids,
    seq_lengths,
    mlm_rows,
    mlm_labels,
    sop_labels,
):
    own = lax.axis_index(AXES)
    words = word_table.shape[0]
    slots = mlm_labels.shape[0]
    pieces = split_vectors(vectors)
    token_kind, allowed = row_layout(seq_lengths)

    facts = jnp.concatenate([token_ids, mlm_labels, seq_lengths])
    padded = -(-facts.shape[0] // 1024) * 1024
    facts = jnp.pad(facts, (0, padded - facts.shape[0])).reshape(-1, 128)
    (all_facts,) = gather_rows([facts])
    all_facts = all_facts.reshape(-1, padded)
    devices = all_facts.shape[0]
    all_ids = all_facts[:, :ROWS].reshape(-1)
    all_labels = all_facts[:, ROWS : ROWS + slots].reshape(-1)
    all_seconds = all_facts[:, ROWS + slots + 1] > 0
    all_used = (all_labels >= 0).astype(jnp.float32)
    mlm_count = jnp.sum(all_used)
    sop_count = devices + jnp.sum(all_seconds.astype(jnp.float32))
    scales = (1.0 / mlm_count, 1.0 / sop_count)

    word_half = to_half(word_table)
    wide, tall, head, place = gather_rows(
        [
            to_half(layer_wide).T,
            to_half(layer_tall),
            to_half(head_weights).T,
            to_half(position_table),
        ]
    )

    offset = own * words
    column = jnp.arange(words, dtype=jnp.int32)
    select = to_half((all_ids - offset)[:, None] == column[None, :])
    (found,) = scatter_rows([to_half(product(select, word_half))])
    two = seq_lengths[1] > 0
    place = place[:ROWS].astype(jnp.float32)
    placed = jnp.concatenate([place[:BUCKET], jnp.where(two, place[:BUCKET], place[BUCKET:])], 0)
    types = pieces["types"].reshape(2, E)
    embedded = (
        found.astype(jnp.float32)
        + placed
        + jnp.where(token_kind[:, None] == 0, types[0:1], types[1:2])
    )
    embed_hat, embed_inverse = norm_forward(embedded)
    normed_half = to_half(embed_hat * pieces["emb_g"] + pieces["emb_b"])
    hidden = product(normed_half, head[E + D :]) + pieces["proj_b"]

    final, kept = lax.scan(
        lambda h, unused: layer_forward(h, wide, tall, pieces, allowed),
        hidden,
        None,
        length=LAYERS,
    )

    final_half = to_half(final)
    pick = to_half(mlm_rows[:, None] == jnp.arange(ROWS, dtype=jnp.int32)[None, :])
    picked = to_half(product(pick, final_half))
    dense = times_transpose(picked, head[:E]) + pieces["mlm_b"]
    mlm_hat, mlm_inverse = norm_forward(gelu_tanh(dense))
    rows_half = to_half(mlm_hat * pieces["mlm_g"] + pieces["mlm_lb"])
    (all_rows,) = gather_rows([rows_half])
    logits = times_transpose(all_rows, word_half) + to_half(decoder_bias).astype(jnp.float32)
    onehot = ((all_labels - offset)[:, None] == column[None, :]).astype(jnp.float32)
    own_top = jnp.max(logits, -1)
    own_total = jnp.sum(jnp.exp(logits - own_top[:, None]), -1)
    own_target = jnp.sum(logits * onehot, -1)
    stats = lax.all_gather(jnp.stack([own_top, own_total, own_target]), AXES)
    top = jnp.max(stats[:, 0], 0)
    total = jnp.sum(stats[:, 1] * jnp.exp(stats[:, 0] - top[None]), 0)
    log_total = jnp.log(total) + top
    mlm_sum = jnp.sum((log_total - jnp.sum(stats[:, 2], 0)) * all_used)
    logits_half = to_half(
        (jnp.exp(logits - top[:, None]) / total[:, None] - onehot) * (all_used * scales[0])[:, None]
    )
    back_decoder = column_sum(logits_half)
    back_word_head = transpose_times(logits_half, all_rows)
    (back_rows,) = scatter_rows([product(logits_half, word_half)])
    back_mlm_g = jnp.sum(back_rows * mlm_hat, 0)
    back_mlm_lb = jnp.sum(back_rows, 0)
    dense_half = to_half(
        norm_backward(back_rows, pieces["mlm_g"], mlm_hat, mlm_inverse) * gelu_slope(dense)
    )
    back_mlm = transpose_times(dense_half, picked)
    back_picked = product(dense_half, head[:E])
    back_final = lax.dot_general(
        pick.astype(jnp.float32), back_picked, (((0,), (0,)), ((), ())), precision=PRECISE
    )

    firsts = jnp.concatenate([final_half[0:1], final_half[BUCKET : BUCKET + 1]], 0)
    pooled = jnp.tanh(times_transpose(firsts, head[E : E + D]) + pieces["pool_b"])
    classifier = pieces["cls"].reshape(2, D)
    classes = jnp.sum(pooled[:, None] * classifier[None], -1)
    class_top = jnp.max(classes, -1, keepdims=True)
    class_powers = jnp.exp(classes - class_top)
    class_totals = jnp.sum(class_powers, -1, keepdims=True)
    class_onehot = (jnp.arange(2, dtype=jnp.int32)[None, :] == sop_labels[:, None]).astype(
        jnp.float32
    )
    present = jnp.stack([jnp.float32(1.0), two.astype(jnp.float32)])
    sop_sum = jnp.sum(
        (jnp.log(class_totals[:, 0]) + class_top[:, 0] - jnp.sum(classes * class_onehot, -1))
        * present
    )
    back_classes = (class_powers / class_totals - class_onehot) * (present * scales[1])[:, None]
    back_cls = jnp.sum(back_classes[:, :, None] * pooled[:, None], 0)
    back_pooled = jnp.sum(back_classes[:, :, None] * classifier[None], 1)
    pre_half = to_half(back_pooled * (1.0 - pooled * pooled))
    back_pool = transpose_times(pre_half, firsts)
    back_firsts = product(pre_half, head[E : E + D])
    row_index = jnp.arange(ROWS, dtype=jnp.int32)[:, None]
    back_final = (
        back_final
        + jnp.where(row_index == 0, back_firsts[0:1], 0.0)
        + jnp.where(row_index == BUCKET, back_firsts[1:2], 0.0)
    )

    back_hidden, back = lax.scan(
        lambda up, k: layer_backward(up, k, wide, tall, pieces), back_final, kept, reverse=True
    )

    upstream_half = to_half(back_hidden)
    back_normed = times_transpose(upstream_half, head[E + D :])
    back_proj = transpose_times(normed_half, upstream_half)
    back_embedded = norm_backward(back_normed, pieces["emb_g"], embed_hat, embed_inverse)
    (all_back,) = gather_rows([to_half(back_embedded)])
    back_word = back_word_head + transpose_times(select, all_back)
    places = position_table.shape[0]
    by_device = all_back.reshape(devices, ROWS, E)
    folded = by_device[:, :BUCKET].astype(jnp.float32) + jnp.where(
        all_seconds[:, None, None], by_device[:, BUCKET:].astype(jnp.float32), 0.0
    )
    rest = jnp.where(all_seconds[:, None, None], 0.0, by_device[:, BUCKET:].astype(jnp.float32))
    all_place = jnp.concatenate([jnp.sum(folded, 0), jnp.sum(rest, 0)], 0)
    all_place = jnp.pad(all_place, ((0, places * devices - ROWS), (0, 0)))
    back_place = lax.dynamic_slice(all_place, (own * places, 0), (places, E))

    def long(x):
        return x.reshape(-1, x.shape[-1])

    joint_all, branch_all = long(back["joint_half"]), long(back["branch_half"])
    inner_all, outer_all = long(back["inner_half"]), long(back["outer_half"])
    back_wide = jnp.concatenate(
        [
            transpose_times(joint_all, long(kept["hidden_half"])),
            transpose_times(branch_all, long(kept["mixed"])),
            transpose_times(inner_all, long(kept["middle_half"])),
        ],
        0,
    )
    back_tall = transpose_times(long(kept["active"]), outer_all)
    back_head = jnp.concatenate([back_mlm, back_pool, back_proj], 0)
    sum_wide, sum_tall, sum_head = scatter_rows([back_wide, back_tall, back_head])

    joint_sum = column_sum(joint_all)
    norms = jnp.sum(back["norms"], 0)
    kind_one = jnp.sum(jnp.where(token_kind[:, None] == 1, back_embedded, 0.0), 0)
    kind_zero = jnp.sum(jnp.where(token_kind[:, None] == 0, back_embedded, 0.0), 0)
    vector_grad = join_vectors(
        {
            "proj_b": column_sum(upstream_half),
            "q_b": joint_sum[:D],
            "v_b": joint_sum[2 * D :],
            "o_b": column_sum(branch_all),
            "ln1_g": norms[0],
            "ln1_b": norms[1],
            "ffo_b": column_sum(outer_all),
            "ln2_g": norms[2],
            "ln2_b": norms[3],
            "pool_b": column_sum(pre_half),
            "cls": back_cls,
            "ff_b": column_sum(inner_all),
            "emb_g": jnp.sum(back_normed * embed_hat, 0),
            "emb_b": jnp.sum(back_normed, 0),
            "mlm_b": column_sum(dense_half),
            "mlm_g": back_mlm_g,
            "mlm_lb": back_mlm_lb,
            "types": jnp.concatenate([kind_zero, kind_one]),
        }
    )
    shards = (back_word, back_place, sum_head.T, back_decoder, sum_wide.T, sum_tall)
    local_squares = jnp.sum(jnp.stack([jnp.sum(s * s) for s in shards]))
    reduced, sop_total, squares = lax.psum((vector_grad, sop_sum, local_squares), AXES)
    grad_norm = jnp.sqrt(squares + jnp.sum(reduced * reduced))
    factor = jnp.minimum(1.0, CLIP_NORM / (grad_norm + NORM_EPSILON))
    updates = []
    for weight, gradient, first, second, rate in (
        (word_table, shards[0], word_first, word_second, LEARN_RATE),
        (position_table, shards[1], position_first, position_second, LEARN_RATE),
        (head_weights, shards[2], head_first, head_second, LEARN_RATE),
        (decoder_bias, shards[3], decoder_first, decoder_second, LEARN_RATE),
        (layer_wide, shards[4], wide_first, wide_second, LEARN_RATE),
        (layer_tall, shards[5], tall_first, tall_second, LEARN_RATE),
        (vectors, reduced, vector_first, vector_second, SMALL_RATE),
    ):
        updates.extend(adam_update(weight, factor * gradient, first, second, rate))
    return (*updates, mlm_sum, mlm_count, sop_total, sop_count, grad_norm)


def solution(mesh):
    rows = P(AXES, None)
    columns = P(None, AXES)
    flat = P(AXES)
    whole = P()
    return jax.shard_map(
        local,
        mesh=mesh,
        in_specs=(rows, rows, columns, flat, columns, rows, whole)
        + (rows, rows) * 2
        + (columns, columns, flat, flat, columns, columns, rows, rows, whole, whole)
        + (flat,) * 5,
        out_specs=(rows,) * 6
        + (columns,) * 3
        + (flat,) * 3
        + (columns,) * 3
        + (rows,) * 3
        + (whole,) * 8,
        check_vma=False,
    )
```

time: 3530 us -> 1460 us (0.41)
  waiting for transfers between devices: 2780 us -> 861 us
  matrix products: 274 us -> 182 us
  local copies, waits for them, and re-layouts: 142 us -> 65.2 us
  blocking collectives: 164 us -> 200 us
    all_gather x18 -> x4, waiting for transfers between devices: 1140 us -> 206 us  [gather_rows(): return [lax.all_gather(s, AXES, axis=0, tiled=True) for s in shards]]
    while x28 -> x0, waiting for transfers between devices: 852 us -> none
    reduce_scatter x7 -> x4, waiting for transfers between devices: 702 us -> 527 us  [scatter_rows(): lax.psum_scatter(s, AXES, scatter_dimension=0, tiled=True)]
    all_gather x1 -> x4, blocking collectives: 40.6 us -> 159 us  [the longest x3 121 us: gather_rows(): return [lax.all_gather(s, AXES, axis=0, tiled=True) for s in shards]]
    while x489 -> x104, local copies, waits for them, and re-layouts: 109 us -> 12.1 us
    dot_general x32 -> x22, matrix products: 111 us -> 49 us  [product(): return jnp.dot(a, b, preferred_element_type=jnp.float32)]
    unnamed x1 -> x0, blocking collectives: 42.9 us -> none
    psum x2 -> x1, blocking collectives: 80.5 us -> 40.1 us  [local(): lax.psum((vector_grad, sop_sum, local_squares), AXES)]
  transfers between devices with their start and end apart: 30 -> 9, of which waited for: 29 -> 9; matrix products, arithmetic and copies ran while one was open for 11% -> 5% of each run, Pallas kernels for 0% -> 0%
where the time goes in v1:
time: 1460 us; the launch traced here: 1450 us
  waiting for transfers between devices  861 us (59%)
  blocking collectives  200 us (14%)
  matrix products  182 us (12%)
  other arithmetic  115 us (8%)
  local copies, waits for them, and re-layouts  65.2 us (4%)
  between operations  25.2 us (2%)
    reduce_scatter x4, waiting for transfers between devices, scatter_rows(): lax.psum_scatter(s, AXES, scatter_dimension=0, tiled=True)  527 us
    all_gather x4, waiting for transfers between devices, gather_rows(): return [lax.all_gather(s, AXES, axis=0, tiled=True) for s in shards]  206 us
    unnamed x10, waiting for transfers between devices  128 us
    all_gather x3, blocking collectives, gather_rows(): return [lax.all_gather(s, AXES, axis=0, tiled=True) for s in shards]  121 us
    dot_general x20, matrix products, times_transpose(): lax.dot_general(a, b, (((1,), (1,)), ((), ())), preferred_element_type=jn...  66.8 us
    dot_general x22, matrix products, product(): return jnp.dot(a, b, preferred_element_type=jnp.float32)  49 us
    psum x1, blocking collectives, local(): lax.psum((vector_grad, sop_sum, local_squares), AXES)  40.1 us
    all_gather x1, blocking collectives, local(): stats = lax.all_gather(jnp.stack([own_top, own_total, own_target]), AXES)  38.4 us
  transfers between devices with their start and end apart: 9, of which 9 were waited for; matrix products, arithmetic and copies ran while one was open for 5% of the time, Pallas kernels for 0%

profile of v1, /device:TPU:0, one launch (start us, length us, event | category | flops | bytes accessed | tf_op | source)
XLA Modules:
  0.0 1450.5 jit_solution(6119171533400283841)
XLA Ops:
  8.0 43.5 %all_gather.27 = s32[256,128]{1,0:T(8,128)S(1)} all-gather(s32[8,128]{1,0:T(8,128)S(1)} %pad_bitcast_fusion), channel_id=1, replica_groups=mesh['dp'=4,'fsdp'=8] {'dp','fsdp'}, dimensions={0}, use_global_device_ids=true | all-gather | bytes 135168 | tf_op jit(solution)/shard_map/all_gather | solution.py:130
  51.7 11.1 fusion.76
  68.3 37.3 %all_gather.28 = bf16[512,128]{1,0:T(8,128)(2,1)S(1)} all-gather(bf16[16,128]{1,0:T(8,128)(2,1)S(1)} %convert_element_type.256), channel_id=1, replica_groups=mesh['dp'=4,'fsdp'=8] {'dp','fsdp'}, dimensions={0}, use_global_device_ids=true | all-gather | bytes 135168 | tf_op jit(solution)/shard_map/all_gather | solution.py:130
  111.0 84.8 %reduce-scatter.9.cloned.1.call-done = bf16[256,128]{1,0:T(8,128)(2,1)} async-done(((bf16[8192,128]{1,0:T(8,128)(2,1)}), bf16[256,128]{1,0:T(8,128)(2,1)}) %reduce-scatter.9.cloned.1.call-update) | async-done | bytes 65552 | tf_op jit(solution)/shard_map/reduce_scatter | solution.py:134
  197.0 53.4 %all-gather.7.cloned.1.call-done = bf16[1024,768]{1,0:T(8,128)(2,1)} async-done(((bf16[32,768]{1,0:T(8,128)(2,1)}), bf16[1024,768]{1,0:T(8,128)(2,1)}) %all-gather.7.cloned.1.call-update) | async-done | bytes 1572880 | tf_op jit(solution)/shard_map/all_gather | solution.py:130
  251.7 65.2 %all-gather.11.cloned.1.call-done = bf16[3072,768]{1,0:T(8,128)(2,1)} async-done(((bf16[96,768]{1,0:T(8,128)(2,1)}), bf16[3072,768]{1,0:T(8,128)(2,1)}) %all-gather.11.cloned.1.call-update) | async-done | bytes 4718608 | tf_op jit(solution)/shard_map/all_gather | solution.py:130
  316.9 84.6 %all-gather.9.cloned.1.call-done = bf16[6144,768]{1,0:T(8,128)(2,1)} async-done(((bf16[192,768]{1,0:T(8,128)(2,1)}), bf16[6144,768]{1,0:T(8,128)(2,1)}) %all-gather.9.cloned.1.call-update) | async-done | bytes 9437200 | tf_op jit(solution)/shard_map/all_gather | solution.py:130
  407.5 94.6 %while.58 = (s32[]{:T(128)}, f32[256,768]{1,0:T(8,128)S(1)}, bf16[4,256,3072]{2,1,0:T(8,128)(2,1)}, f32[4,256,768]{2,1,0:T(8,128)}, f32[4,256,768]{2,1,0:T(8,128...) while((s32[]{:T(128)}, f32[256,768]{1,0:T(8,128)S(1)}, ...), condition=%wide.region_10.11_spmd.clone, body=%wide.region_3.0_spmd.clone.sunk | while | flops 3855815936 | bytes 110778992 | solution.py:307
  504.0 40.2 %all_gather.32 = bf16[1280,128]{1,0:T(8,128)(2,1)S(1)} all-gather(bf16[40,128]{1,0:T(8,128)(2,1)S(1)} %add_convert_fusion.1), channel_id=1, replica_groups=mesh['dp'=4,'fsdp'=8] {'dp','fsdp'}, dimensions={0}, use_global_device_ids=true | all-gather | bytes 337920 | tf_op jit(solution)/shard_map/all_gather | solution.py:130
  550.3 38.4 %all-gather.1 = f32[32,3,1280]{2,1,0:T(4,128)S(1)} all-gather(f32[1,3,1280]{2,1,0:T(4,128)S(1)} %maximum_bitcast_fusion.1), channel_id=2, replica_groups=mesh['dp'=4,'fsdp'=8] {'dp','fsdp'}, dimensions={0}, use_global_device_ids=true | all-gather | bytes 506880 | tf_op jit(solution)/shard_map/all_gather | solution.py:326
  602.8 128.3 %reduce-scatter.17.cloned.1.call-done = f32[40,128]{1,0:T(8,128)} async-done(((f32[1280,128]{1,0:T(8,128)}), f32[40,128]{1,0:T(8,128)}) %reduce-scatter.17.cloned.1.call-update) | async-done | bytes 20496
  743.2 126.4 %while.57 = (s32[]{:T(128)}, f32[256,768]{1,0:T(8,128)S(1)}, bf16[4,256,768]{2,1,0:T(8,128)(2,1)S(1)}, bf16[4,256,3072]{2,1,0:T(8,128)(2,1)}, bf16[4,256,2304]{1...) while((s32[]{:T(128)}, f32[256,768]{1,0:T(8,128)S(1)}, ...), condition=%wide.region_37.38_spmd, body=%wide.region_27.37_spmd.sunk | while | flops 4053470208 | bytes 122044864 | solution.py:376
  747.6 7.4 bitcast_dynamic-update-slice_fusion.21
  779.1 7.4 bitcast_dynamic-update-slice_fusion.21
  810.6 7.5 bitcast_dynamic-update-slice_fusion.21
  842.3 7.5 bitcast_dynamic-update-slice_fusion.21
  877.7 10.0 convolution_bitcast_fusion
  890.8 5.9 convolution_bitcast_fusion.2
  901.9 7.4 pad_maximum_fusion.1
  929.4 8.5 multiply_reduce_fusion.5
  939.2 92.6 %reduce-scatter.11.cloned.1.call-done = f32[32,768]{1,0:T(8,128)} async-done(((f32[1024,768]{1,0:T(8,128)}), f32[32,768]{1,0:T(8,128)}) %reduce-scatter.11.cloned.1.call-update) | async-done | bytes 98320 | tf_op jit(solution)/shard_map/reduce_scatter | solution.py:134
  1034.7 137.7 %reduce-scatter.15.cloned.1.call-done = f32[96,768]{1,0:T(8,128)} async-done(((f32[3072,768]{1,0:T(8,128)}), f32[96,768]{1,0:T(8,128)}) %reduce-scatter.15.cloned.1.call-update) | async-done | bytes 294928 | tf_op jit(solution)/shard_map/reduce_scatter | solution.py:134
  1174.1 211.6 %reduce-scatter.13.cloned.1.call-done = f32[192,768]{1,0:T(8,128)} async-done(((f32[6144,768]{1,0:T(8,128)}), f32[192,768]{1,0:T(8,128)}) %reduce-scatter.13.cloned.1.call-update) | async-done | bytes 589840 | tf_op jit(solution)/shard_map/reduce_scatter | solution.py:134
  1389.0 40.1 %all-reduce.3 = (f32[]{:T(128)}, f32[13184]{0:T(1024)S(1)}, f32[]{:T(128)}) all-reduce(f32[]{:T(128)S(6)} %reduce_sum.633, f32[13184]{0:T(1024)} %copy-done.41, f32[]{:T(128)} %select_reduce_fusion.5), channel_id=1, replica_groups=mesh['dp'=4,'fsdp'=8] {'dp','fsdp'}, use_global_device_ids=true, to_apply=%region_52.53 | all-reduce | flops 13186 | bytes 105488 | tf_op jit(solution)/shard_map/psum | solution.py:441
  (628 shorter events, 293.7 us)
Async XLA Ops:
  7.2 188.5 %reduce-scatter.9.cloned.1.call-start = ((), (), s32[]{:S(2)}) async-start(), calls=%async_computation.5 | async-start | bytes 2162688 | tf_op jit(solution)/shard_map/reduce_scatter | solution.py:134
  62.9 187.5 %all-gather.7.cloned.1.call-start = ((), (), s32[]{:S(2)}) async-start(), calls=%async_computation.6 | async-start | bytes 1622016 | tf_op jit(solution)/shard_map/all_gather | solution.py:130
  63.7 253.2 %all-gather.11.cloned.1.call-start = ((), (), s32[]{:S(2)}) async-start(), calls=%async_computation.8 | async-start | bytes 4866048 | tf_op jit(solution)/shard_map/all_gather | solution.py:130
  64.4 337.1 %all-gather.9.cloned.1.call-start = ((), (), s32[]{:S(2)}) async-start(), calls=%async_computation.7 | async-start | bytes 9732096 | tf_op jit(solution)/shard_map/all_gather | solution.py:130
  65.3 665.8 %reduce-scatter.17.cloned.1.call-start = ((), (), s32[]{:S(2)}) async-start(), calls=%async_computation.13 | async-start | bytes 675840
  108.5 296.4 %copy-start.63 = (pred[256]{0:T(512)(128)(4,1)}, pred[256]{0:T(512)(128)(4,1)S(1)}, u32[]{:S(2)}) copy-start(pred[256]{0:T(512)(128)(4,1)S(1)} %get-tuple-element.1133) | copy-start | bytes 772
  110.3 294.6 %copy-start.57 = (f32[128]{0:T(128)}, f32[128]{0:T(128)S(1)}, u32[]{:S(2)}) copy-start(f32[128]{0:T(128)S(1)} %get-tuple-element.1118) | copy-start | bytes 1540
  110.3 294.6 %copy-start.61 = (f32[128]{0:T(128)}, f32[128]{0:T(128)S(1)}, u32[]{:S(2)}) copy-start(f32[128]{0:T(128)S(1)} %get-tuple-element.1117) | copy-start | bytes 1540
  196.8 208.2 %copy-start.9 = (f32[256,128]{1,0:T(8,128)}, f32[256,128]{1,0:T(8,128)S(1)}, u32[]{:S(2)}) copy-start(f32[256,128]{1,0:T(8,128)S(1)} %get-tuple-element.1068) | copy-start | bytes 393220
  196.8 208.2 %copy-start.43 = (f32[256]{0:T(256)}, f32[256]{0:T(256)S(1)}, u32[]{:S(2)}) copy-start(f32[256]{0:T(256)S(1)} %broadcast_multiply_fusion.8) | copy-start | bytes 3076
  197.0 208.0 %copy-start.51 = (f32[256]{0:T(256)}, f32[256]{0:T(256)S(1)}, u32[]{:S(2)}) copy-start(f32[256]{0:T(256)S(1)} %add_rsqrt_fusion.2) | copy-start | bytes 3076
  598.7 135.2 %copy-start.79 = (pred[256]{0:T(512)(128)(4,1)S(1)}, pred[256]{0:T(512)(128)(4,1)}, u32[]{:S(2)}) copy-start(pred[256]{0:T(512)(128)(4,1)} %get-tuple-element.1136) | copy-start | bytes 772
  598.7 135.2 %copy-start.80 = (pred[256]{0:T(512)(128)(4,1)S(1)}, pred[256]{0:T(512)(128)(4,1)}, u32[]{:S(2)}) copy-start(pred[256]{0:T(512)(128)(4,1)} %get-tuple-element.1137) | copy-start | bytes 772
  598.7 327.3 %all-gather.13.cloned.1.call-start = ((), (), s32[]{:S(2)}) async-start(), calls=%async_computation.9 | async-start | bytes 2162688 | tf_op jit(solution)/shard_map/all_gather | solution.py:130
  599.9 138.8 %copy-start.59 = (f32[2]{0:T(128)}, f32[2]{0:T(128)S(1)}, u32[]{:S(2)}) copy-start(f32[2]{0:T(128)S(1)} %reduce_max.38) | copy-start | bytes 28
  602.4 129.9 %copy-start.50 = (bf16[2,768]{1,0:T(2,128)(2,1)}, bf16[2,768]{1,0:T(2,128)(2,1)S(1)}, u32[]{:S(2)}) copy-start(bf16[2,768]{1,0:T(2,128)(2,1)S(1)} %get-tuple-element.1061) | copy-start | bytes 9220
  873.5 158.3 %reduce-scatter.11.cloned.1.call-start = ((), (), s32[]{:S(2)}) async-start(), calls=%async_computation.10 | async-start | bytes 3244032 | tf_op jit(solution)/shard_map/reduce_scatter | solution.py:134
  877.5 294.9 %reduce-scatter.15.cloned.1.call-start = ((), (), s32[]{:S(2)}) async-start(), calls=%async_computation.12 | async-start | bytes 9732096 | tf_op jit(solution)/shard_map/reduce_scatter | solution.py:134
  887.7 498.0 %reduce-scatter.13.cloned.1.call-start = ((), (), s32[]{:S(2)}) async-start(), calls=%async_computation.11 | async-start | bytes 19464192 | tf_op jit(solution)/shard_map/reduce_scatter | solution.py:134
  929.4 501.7 %copy-start.31 = (f32[13184]{0:T(1024)S(1)}, f32[13184]{0:T(1024)}, u32[]{:S(2)}) copy-start(f32[13184]{0:T(1024)} %param.36) | copy-start | bytes 158212
  929.4 503.3 %copy-start.55 = (f32[960]{0:T(1024)S(1)}, f32[960]{0:T(1024)}, u32[]{:S(2)}) copy-start(f32[960]{0:T(1024)} %param.33) | copy-start | bytes 11524
  929.4 506.0 %copy-start.12 = (f32[960,128]{1,0:T(8,128)S(1)}, f32[960,128]{1,0:T(8,128)}, u32[]{:S(2)}) copy-start(f32[960,128]{1,0:T(8,128)} %param.30) | copy-start | bytes 1474564
  937.9 500.2 %copy-start.21 = (f32[96,768]{1,0:T(8,128)S(1)}, f32[96,768]{1,0:T(8,128)}, u32[]{:S(2)}) copy-start(f32[96,768]{1,0:T(8,128)} %param.35) | copy-start | bytes 884740
  1172.4 265.7 %copy-start.22 = (f32[96,768]{1,0:T(8,128)S(1)}, f32[96,768]{1,0:T(8,128)}, u32[]{:S(2)}) copy-start(f32[96,768]{1,0:T(8,128)} %reduce-scatter.15.cloned.1.call-done) | copy-start | bytes 884740
  (116 other events, 1314.7 us)
Sparse Core Ops, SparseCore 0:
  63.0 132.6 reduce-scatter.8
  199.6 50.8 all-gather.6
  254.3 62.5 all-gather.10
  320.6 80.8 all-gather.8
  598.8 132.1 reduce-scatter.16
  873.6 52.3 all-gather.12
  931.4 100.3 reduce-scatter.10
  1037.7 134.5 reduce-scatter.14
  1179.9 205.7 reduce-scatter.12

commit v2 on v1

--- a/solution.py
+++ b/solution.py
@@ -1,6 +1,10 @@
+import functools
+
 import jax
 import jax.numpy as jnp
 from jax import lax
+from jax.experimental import pallas as pl
+from jax.experimental.pallas import tpu as pltpu
 from jax.sharding import PartitionSpec as P
 
 D = 768
@@ -126,12 +130,678 @@
     return (token_kind, allowed)
 
 
-def gather_rows(shards):
-    return [lax.all_gather(s, AXES, axis=0, tiled=True) for s in shards]
-
-
-def scatter_rows(partials):
-    return [lax.psum_scatter(s, AXES, scatter_dimension=0, tiled=True) for s in partials]
+MESH_ID = pl.DeviceIdType.MESH
+VMEM_SPACE = pltpu.VMEM
+VMEM_ASK = 60 * 1024 * 1024
+
+
+def greet(peers):
+    barrier = pltpu.get_barrier_semaphore()
+    count = 0
+    for present, who in peers:
+        if present is None:
+            pl.semaphore_signal(barrier, inc=1, device_id=who, device_id_type=MESH_ID)
+            count = count + 1
+        else:
+
+            @pl.when(present)
+            def _(who=who):
+                pl.semaphore_signal(barrier, inc=1, device_id=who, device_id_type=MESH_ID)
+
+            count = count + present.astype(jnp.int32)
+    pl.semaphore_wait(barrier, count)
+
+
+def maybe(condition, action):
+    if condition is None:
+        action()
+    else:
+        pl.when(condition)(action)
+
+
+def remote(source, target, send, receive, who):
+    return pltpu.make_async_remote_copy(
+        src_ref=source,
+        dst_ref=target,
+        send_sem=send,
+        recv_sem=receive,
+        device_id=who,
+        device_id_type=MESH_ID,
+    )
+
+
+def small_gather_kernel(count, planes, width, *refs):
+    ins, outs = refs[:count], refs[count : 2 * count]
+    send_z, recv_z, send_f, recv_f = refs[2 * count :]
+    z, f = lax.axis_index("dp"), lax.axis_index("fsdp")
+    line = [(lax.rem(z + d, planes), f) for d in range(1, planes)]
+    plane = [(z, lax.rem(f + d, width)) for d in range(1, width)]
+    greet([(None, who) for who in line + plane])
+    first = [
+        remote(ins[i], outs[i].at[z, f], send_z.at[i, d], recv_z.at[i, d], who)
+        for d, who in enumerate(line)
+        for i in range(count)
+    ]
+    for copy in first:
+        copy.start()
+    for i in range(count):
+        outs[i][z, f] = ins[i][...]
+    for copy in first:
+        copy.wait_recv()
+    second = [
+        remote(outs[i].at[:, f], outs[i].at[:, f], send_f.at[i, d], recv_f.at[i, d], who)
+        for d, who in enumerate(plane)
+        for i in range(count)
+    ]
+    for copy in second:
+        copy.start()
+    for d in range(1, width):
+        other = lax.rem(f - d + width, width)
+        for i in range(count):
+            remote(
+                outs[i].at[:, other],
+                outs[i].at[:, other],
+                send_f.at[i, d - 1],
+                recv_f.at[i, d - 1],
+                (z, f),
+            ).wait_recv()
+    for copy in first + second:
+        copy.wait_send()
+
+
+def small_gather(arrays, mesh_shape, identity):
+    planes, width = mesh_shape
+    count = len(arrays)
+    return pl.pallas_call(
+        functools.partial(small_gather_kernel, count, planes, width),
+        out_shape=[
+            jax.ShapeDtypeStruct((planes, width, *a.shape), a.dtype) for a in arrays
+        ],
+        in_specs=[pl.BlockSpec(memory_space=VMEM_SPACE)] * count,
+        out_specs=[pl.BlockSpec(memory_space=VMEM_SPACE)] * count,
+        scratch_shapes=[
+            pltpu.SemaphoreType.DMA((count, planes)),
+            pltpu.SemaphoreType.DMA((count, planes)),
+            pltpu.SemaphoreType.DMA((count, width)),
+            pltpu.SemaphoreType.DMA((count, width)),
+        ],
+        compiler_params=pltpu.CompilerParams(
+            collective_id=identity, has_side_effects=True, vmem_limit_bytes=VMEM_ASK
+        ),
+    )(*arrays)
+
+
+def small_scatter_kernel(planes, width, x, out, first_in, middle, second_in, *sems):
+    send_f, recv_f, send_z, recv_z = sems
+    z, f = lax.axis_index("dp"), lax.axis_index("fsdp")
+    line = [(lax.rem(z + d, planes), f) for d in range(1, planes)]
+    plane = [(z, lax.rem(f + d, width)) for d in range(1, width)]
+    greet([(None, who) for who in line + plane])
+    first = [
+        remote(x.at[:, who[1]], first_in.at[d], send_f.at[d], recv_f.at[d], who)
+        for d, who in enumerate(plane)
+    ]
+    for copy in first:
+        copy.start()
+    total = x[:, f]
+    for d, copy in enumerate(first):
+        copy.wait_recv()
+        total = total + first_in[d]
+    middle[...] = total
+    second = [
+        remote(middle.at[who[0]], second_in.at[d], send_z.at[d], recv_z.at[d], who)
+        for d, who in enumerate(line)
+    ]
+    for copy in second:
+        copy.start()
+    total = middle[z]
+    for d, copy in enumerate(second):
+        copy.wait_recv()
+        total = total + second_in[d]
+    out[...] = total
+    for copy in first + second:
+        copy.wait_send()
+
+
+def small_scatter(x, mesh_shape, identity):
+    planes, width = mesh_shape
+    block = x.shape[2:]
+    return pl.pallas_call(
+        functools.partial(small_scatter_kernel, planes, width),
+        out_shape=jax.ShapeDtypeStruct(block, x.dtype),
+        in_specs=[pl.BlockSpec(memory_space=VMEM_SPACE)],
+        out_specs=pl.BlockSpec(memory_space=VMEM_SPACE),
+        scratch_shapes=[
+            VMEM_SPACE((width - 1, planes, *block), x.dtype),
+            VMEM_SPACE((planes, *block), x.dtype),
+            VMEM_SPACE((planes - 1, *block), x.dtype),
+            pltpu.SemaphoreType.DMA((width - 1,)),
+            pltpu.SemaphoreType.DMA((width - 1,)),
+            pltpu.SemaphoreType.DMA((planes - 1,)),
+            pltpu.SemaphoreType.DMA((planes - 1,)),
+        ],
+        compiler_params=pltpu.CompilerParams(
+            collective_id=identity, has_side_effects=True, vmem_limit_bytes=VMEM_ASK
+        ),
+    )(x)
+
+
+OWN, ACROSS_X, ACROSS_Y, DIAGONAL = 0, 1, 2, 3
+
+
+def cuts_of(rows):
+    tail = max(32, round(rows * 0.22 / 32) * 32)
+    head = rows - tail
+    return ((0, head), (head, rows))
+
+
+def half_of(span, which):
+    low, high = span
+    middle = (low + high) // 2
+    return (low, middle) if which == 0 else (middle, high)
+
+
+def places():
+    z, f = lax.axis_index("dp"), lax.axis_index("fsdp")
+    q, c = f // 2, lax.rem(f, 2)
+    qx = q + 1 - 2 * lax.rem(q, 2)
+    qy = lax.rem(q + 2, 4)
+    qd = qx + qy - q
+    return z, c, (q, qx, qy, qd)
+
+
+def big_gather_kernel(planes, rows, members, x, *refs):
+    outs = refs[: len(members)]
+    buf, out_sem, send, recv, side_send, side_recv = refs[len(members) :]
+    z, c, cols = places()
+    cuts = cuts_of(rows)
+    at_x, at_y, mate = (z, cols[1] * 2 + c), (z, cols[2] * 2 + c), (z, cols[0] * 2 + 1 - c)
+    above, below = z < planes - 1, z > 0
+    up, down = (z + 1, cols[0] * 2 + c), (z - 1, cols[0] * 2 + c)
+    greet([(None, at_x), (None, at_y), (None, mate), (above, up), (below, down)])
+    sent = []
+
+    def block(zs, col, core, span):
+        return buf.at[zs, cols[col], core, pl.ds(span[0], span[1] - span[0])]
+
+    def push(condition, zs, col, span, who, slot, receive, mine=False):
+        def make():
+            here = block(zs, col, c, span)
+            source = x.at[pl.ds(span[0], span[1] - span[0])] if mine else here
+            return remote(source, here, send.at[slot[0], zs, slot[1]], receive, who)
+
+        maybe(condition, lambda: make().start())
+        sent.append((condition, make))
+
+    def await_block(zs, col, span, receive, core=None):
+        here = block(zs, col, c if core is None else core, span)
+        remote(here, here, send.at[0, 0, 0], receive, mate).wait_recv()
+
+    def deliver(zs, col, core, span):
+        for index, (out, (low, high)) in enumerate(zip(outs, members)):
+            first, last = max(low, span[0]), min(high, span[1])
+            if first < last:
+                pltpu.make_async_copy(
+                    buf.at[zs, cols[col], core, pl.ds(first, last - first)],
+                    out.at[zs, cols[col], core, pl.ds(first - low, last - first)],
+                    out_sem.at[index],
+                ).start()
+
+    def share(condition, part, zs, col, span, kind, mine=False):
+        def make():
+            here = block(zs, col, c, span)
+            source = x.at[pl.ds(span[0], span[1] - span[0])] if mine else here
+            return remote(
+                source, here, side_send.at[part, zs, kind], side_recv.at[part, zs, kind], mate
+            )
+
+        def action():
+            make().start()
+            if not mine:
+                deliver(zs, col, c, span)
+
+        maybe(condition, action)
+        sent.append((condition, make))
+        shared.append((condition, part, zs, col, span, kind))
+
+    shared = []
+    whole = [cuts[0], cuts[1]]
+    for part in (1, 0):
+        push(None, z, OWN, whole[part], at_x, (part, 0), recv.at[part, z, ACROSS_X], True)
+        push(None, z, OWN, whole[part], at_y, (part, 1), recv.at[part, z, ACROSS_Y], True)
+    for part in (0, 1):
+        push(above, z, OWN, whole[part], up, (part, 2), recv.at[part, z, OWN], True)
+        push(below, z, OWN, whole[part], down, (part, 3), recv.at[part, z, OWN], True)
+    for part in (0, 1):
+        share(None, part, z, OWN, whole[part], 0, True)
+    own_copy = pltpu.make_async_copy(x, buf.at[z, cols[0], c], out_sem.at[len(members)])
+    own_copy.start()
+
+    def turn(condition, part, zs):
+        span = whole[part]
+        for col, which, who, slot in ((ACROSS_X, 1, at_y, 4), (ACROSS_Y, 0, at_x, 5)):
+            maybe(
+                condition,
+                lambda col=col: await_block(zs, col, span, recv.at[part, zs, col]),
+            )
+            push(condition, zs, col, half_of(span, which), who, (part, slot), recv.at[part, zs, 4 + which])
+            if part == 1:
+                push(above, zs, col, span, up, (1, 4 + 2 * col), recv.at[1, zs, col])
+                push(below, zs, col, span, down, (1, 5 + 2 * col), recv.at[1, zs, col])
+            share(condition, part, zs, col, span, col)
+
+    turn(None, 1, z)
+    turn(None, 0, z)
+    for which in (0, 1):
+        await_block(z, DIAGONAL, half_of(whole[1], which), recv.at[1, z, 4 + which])
+    push(above, z, DIAGONAL, whole[1], up, (1, 10), recv.at[1, z, DIAGONAL])
+    push(below, z, DIAGONAL, whole[1], down, (1, 11), recv.at[1, z, DIAGONAL])
+    share(None, 1, z, DIAGONAL, whole[1], 3)
+
+    def settle(upto):
+        while len(shared) > upto:
+            condition, part, zs, col, span, kind = shared.pop(0)
+
+            def action():
+                await_block(zs, col, span, side_recv.at[part, zs, kind], 1 - c)
+                deliver(zs, col, 1 - c, span)
+
+            maybe(condition, action)
+
+    for step in range(1, planes):
+        ways = ((z - step >= 0, z - step, above, up), (z + step < planes, z + step, below, down))
+        for valid, zs, further, onward in ways:
+            go = jnp.logical_and(valid, further)
+            pl.when(valid)(
+                lambda zs=zs: await_block(zs, OWN, whole[0], recv.at[0, zs, OWN])
+            )
+            push(go, zs, OWN, whole[0], onward, (0, 2), recv.at[0, zs, OWN])
+            push(valid, zs, OWN, whole[0], at_x, (0, 0), recv.at[0, zs, ACROSS_X])
+            push(valid, zs, OWN, whole[0], at_y, (0, 1), recv.at[0, zs, ACROSS_Y])
+            share(valid, 0, zs, OWN, whole[0], 0)
+        waiting = len(shared)
+        for valid, zs, further, onward in ways:
+            go = jnp.logical_and(valid, further)
+            for col in (OWN, ACROSS_X, ACROSS_Y, DIAGONAL):
+                pl.when(valid)(
+                    lambda zs=zs, col=col: await_block(zs, col, whole[1], recv.at[1, zs, col])
+                )
+                push(go, zs, col, whole[1], onward, (1, col), recv.at[1, zs, col])
+                share(valid, 1, zs, col, whole[1], col)
+        for valid, zs, further, onward in ways:
+            turn(valid, 0, zs)
+        settle(8)
+    own_copy.wait()
+    deliver(z, OWN, c, (0, rows))
+    everywhere = [(None, z)] + [
+        (valid, zs)
+        for step in range(1, planes)
+        for valid, zs in ((z - step >= 0, z - step), (z + step < planes, z + step))
+    ]
+    for condition, zs in everywhere:
+        for which in (0, 1):
+            span = half_of(whole[0], which)
+            maybe(
+                condition,
+                lambda zs=zs, which=which, span=span: await_block(
+                    zs, DIAGONAL, span, recv.at[0, zs, 4 + which]
+                ),
+            )
+            share(condition, 0, zs, DIAGONAL, span, 3 + which)
+    settle(0)
+    for condition, make in sent:
+        maybe(condition, lambda make=make: make().wait_send())
+    for index, (out, (low, high)) in enumerate(zip(outs, members)):
+        pltpu.make_async_copy(
+            buf.at[:, :, :, pl.ds(low, high - low)], out, out_sem.at[index]
+        ).wait()
+
+
+def big_gather(x, heights, mesh_shape, identity):
+    planes, width = mesh_shape
+    rows, columns = x.shape
+    members, low = [], 0
+    for height in heights:
+        members.append((low, low + height))
+        low += height
+    outs = pl.pallas_call(
+        functools.partial(big_gather_kernel, planes, rows, tuple(members)),
+        out_shape=[
+            jax.ShapeDtypeStruct((planes, width // 2, 2, height, columns), x.dtype)
+            for height in heights
+        ],
+        in_specs=[pl.BlockSpec(memory_space=VMEM_SPACE)],
+        out_specs=[pl.BlockSpec(memory_space=pl.ANY)] * len(heights),
+        scratch_shapes=[
+            VMEM_SPACE((planes, width // 2, 2, rows, columns), x.dtype),
+            pltpu.SemaphoreType.DMA((len(heights) + 1,)),
+            pltpu.SemaphoreType.DMA((2, planes, 12)),
+            pltpu.SemaphoreType.DMA((2, planes, 6)),
+            pltpu.SemaphoreType.DMA((2, planes, 5)),
+            pltpu.SemaphoreType.DMA((2, planes, 5)),
+        ],
+        compiler_params=pltpu.CompilerParams(
+            collective_id=identity, has_side_effects=True, vmem_limit_bytes=VMEM_ASK
+        ),
+    )(x)
+    return [out.reshape(-1, columns) for out in outs]
+
+
+def accumulate(target, sources, height):
+    step = 32
+
+    def body(i, unused):
+        rows = pl.ds(pl.multiple_of(i * step, step), step)
+        total = sources[0][rows].astype(jnp.float32)
+        for source in sources[1:]:
+            total = total + source[rows].astype(jnp.float32)
+        target[rows] = total.astype(target.dtype)
+        return unused
+
+    lax.fori_loop(0, height // step, body, 0)
+
+
+def big_scatter_kernel(planes, rows, members, *refs):
+    count = len(members)
+    grads, out = refs[:count], refs[count]
+    own, side, half_in, full_in, line_in, tail_line, tail_half, tail_full = refs[
+        count + 1 : count + 9
+    ]
+    load, side_send, side_recv, send, recv, tail_send, tail_recv = refs[count + 9 :]
+    z, c, cols = places()
+    cuts = cuts_of(rows)
+    at_x, at_y, mate = (z, cols[1] * 2 + c), (z, cols[2] * 2 + c), (z, cols[0] * 2 + 1 - c)
+    above, below = z < planes - 1, z > 0
+    up, down = (z + 1, cols[0] * 2 + c), (z - 1, cols[0] * 2 + c)
+    greet([(None, at_x), (None, at_y), (None, mate), (above, up), (below, down)])
+    sent = []
+
+    def push(condition, make):
+        maybe(condition, lambda: make().start())
+        sent.append((condition, make))
+
+    def piece(ref, span):
+        return ref.at[pl.ds(span[0], span[1] - span[0])]
+
+    order = (DIAGONAL, ACROSS_X, ACROSS_Y, OWN)
+    loads = {}
+    for col in order:
+        for a, (low, high) in enumerate(members):
+            copy = pltpu.make_async_copy(
+                grads[a].at[:, cols[col], c],
+                own.at[:, col, pl.ds(low, high - low)],
+                load.at[col, a],
+            )
+            copy.start()
+
+            def make(col=col, a=a, low=low, high=high):
+                return remote(
+                    grads[a].at[:, cols[col], 1 - c],
+                    side.at[:, col, pl.ds(low, high - low)],
+                    side_send.at[col, a],
+                    side_recv.at[col, a],
+                    mate,
+                )
+
+            push(None, make)
+            loads[col, a] = (copy, make)
+
+    def merge(col):
+        for a in range(count):
+            copy, make = loads[col, a]
+            copy.wait()
+            make().wait_recv()
+
+        def body(zt, unused):
+            accumulate(own.at[zt, col], [own.at[zt, col], side.at[zt, col]], rows)
+            return unused
+
+        lax.fori_loop(0, planes, body, 0)
+
+    targets = []
+    for distance in range(planes - 1, 0, -1):
+        targets.append((z + distance < planes, z + distance, 0))
+        targets.append((z - distance >= 0, z - distance, 1))
+    targets.append((None, z, 2))
+    head, tail = cuts
+    height, tail_height = head[1] - head[0], tail[1] - tail[0]
+
+    def half_message(zt, which):
+        return remote(
+            piece(own.at[zt, DIAGONAL], half_of(head, which)),
+            half_in.at[which, zt],
+            send.at[0, which, zt],
+            recv.at[0, which, zt],
+            (at_x, at_y)[which],
+        )
+
+    def full_message(zt, which):
+        return remote(
+            piece(own.at[zt, (ACROSS_X, ACROSS_Y)[which]], head),
+            full_in.at[which, zt],
+            send.at[1, which, zt],
+            recv.at[1, which, zt],
+            (at_x, at_y)[which],
+        )
+
+    def line_message(zt, way):
+        return remote(
+            piece(own.at[zt, OWN], head),
+            line_in.at[way, zt],
+            send.at[2, way, zt],
+            recv.at[2, way, zt],
+            (up, down)[way],
+        )
+
+    def tail_message(zt, way):
+        return remote(
+            own.at[zt, :, pl.ds(tail[0], tail_height)],
+            tail_line.at[way, zt],
+            tail_send.at[way, zt],
+            tail_recv.at[way, zt],
+            (up, down)[way],
+        )
+
+    merge(DIAGONAL)
+    for valid, zt, unused in targets:
+        for which in (0, 1):
+            push(valid, functools.partial(half_message, zt, which))
+    merge(ACROSS_X)
+    merge(ACROSS_Y)
+
+    def second(valid, zt):
+        def add():
+            for which, col in ((1, ACROSS_X), (0, ACROSS_Y)):
+                half_message(zt, which).wait_recv()
+                span = half_of(head, which)
+                target = piece(own.at[zt, col], span)
+                accumulate(target, [target, half_in.at[which, zt]], height // 2)
+
+        maybe(valid, add)
+        for which in (0, 1):
+            push(valid, functools.partial(full_message, zt, which))
+
+    def tail_add(zt, way):
+        tail_message(zt, way).wait_recv()
+        for col in range(4):
+            target = piece(own.at[zt, col], tail)
+            accumulate(target, [target, tail_line.at[way, zt, col]], tail_height)
+
+    def tail_step(valid, zt, way):
+        behind = (below, above)[way]
+        pl.when(jnp.logical_and(valid, behind))(lambda: tail_add(zt, way))
+        push(valid, functools.partial(tail_message, zt, way))
+
+    second(*targets[0][:2])
+    second(*targets[1][:2])
+    merge(OWN)
+    for number in range(2, len(targets)):
+        if number - 2 < len(targets) - 1:
+            tail_step(*targets[number - 2])
+        second(*targets[number][:2])
+    for number in range(len(targets) - 2, len(targets) - 1):
+        tail_step(*targets[number])
+
+    def third(valid, zt, way):
+        def add():
+            for which in (0, 1):
+                full_message(zt, which).wait_recv()
+            base = [piece(own.at[zt, OWN], head), full_in.at[0, zt], full_in.at[1, zt]]
+            behind = (below, above)[way]
+
+            @pl.when(behind)
+            def _():
+                line_message(zt, way).wait_recv()
+                accumulate(base[0], base + [line_in.at[way, zt]], height)
+
+            @pl.when(jnp.logical_not(behind))
+            def _():
+                accumulate(base[0], base, height)
+
+        pl.when(valid)(add)
+        push(valid, functools.partial(line_message, zt, way))
+
+    half_tail = tail_height // 2
+
+    def tail_half_message(which):
+        return remote(
+            piece(own.at[z, DIAGONAL], half_of(tail, which)),
+            tail_half.at[which],
+            tail_send.at[2, which],
+            tail_recv.at[2, which],
+            (at_x, at_y)[which],
+        )
+
+    def tail_full_message(which):
+        return remote(
+            piece(own.at[z, (ACROSS_X, ACROSS_Y)[which]], tail),
+            tail_full.at[which],
+            tail_send.at[3, which],
+            tail_recv.at[3, which],
+            (at_x, at_y)[which],
+        )
+
+    for number, target in enumerate(targets[:-1]):
+        third(*target)
+        if number == len(targets) - 3:
+            pl.when(below)(lambda: tail_add(z, 0))
+            pl.when(above)(lambda: tail_add(z, 1))
+            for which in (0, 1):
+                push(None, functools.partial(tail_half_message, which))
+    for which, col in ((1, ACROSS_X), (0, ACROSS_Y)):
+        tail_half_message(which).wait_recv()
+        target = piece(own.at[z, col], half_of(tail, which))
+        accumulate(target, [target, tail_half.at[which]], half_tail)
+    for which in (0, 1):
+        push(None, functools.partial(tail_full_message, which))
+    for which in (0, 1):
+        full_message(z, which).wait_recv()
+    goal = piece(out, head)
+    accumulate(goal, [piece(own.at[z, OWN], head), full_in.at[0, z], full_in.at[1, z]], height)
+    for present, way in ((below, 0), (above, 1)):
+
+        def add(way=way):
+            line_message(z, way).wait_recv()
+            accumulate(goal, [goal, line_in.at[way, z]], height)
+
+        pl.when(present)(add)
+    for which in (0, 1):
+        tail_full_message(which).wait_recv()
+    accumulate(
+        piece(out, tail),
+        [piece(own.at[z, OWN], tail), tail_full.at[0], tail_full.at[1]],
+        tail_height,
+    )
+    for condition, make in sent:
+        maybe(condition, lambda make=make: make().wait_send())
+
+
+def big_scatter(arrays, mesh_shape, identity):
+    planes, width = mesh_shape
+    columns = arrays[0].shape[1]
+    members, low, views = [], 0, []
+    for a in arrays:
+        height = a.shape[0] // (planes * width)
+        members.append((low, low + height))
+        low += height
+        views.append(a.reshape(planes, width // 2, 2, height, columns))
+    rows = low
+    head, tail = (high - low for low, high in cuts_of(rows))
+    half = arrays[0].dtype
+    return pl.pallas_call(
+        functools.partial(big_scatter_kernel, planes, rows, tuple(members)),
+        out_shape=jax.ShapeDtypeStruct((rows, columns), jnp.float32),
+        in_specs=[pl.BlockSpec(memory_space=pl.ANY)] * len(arrays),
+        out_specs=pl.BlockSpec(memory_space=VMEM_SPACE),
+        scratch_shapes=[
+            VMEM_SPACE((planes, 4, rows, columns), half),
+            VMEM_SPACE((planes, 4, rows, columns), half),
+            VMEM_SPACE((2, planes, head // 2, columns), half),
+            VMEM_SPACE((2, planes, head, columns), half),
+            VMEM_SPACE((2, planes, head, columns), half),
+            VMEM_SPACE((2, planes, 4, tail, columns), half),
+            VMEM_SPACE((2, tail // 2, columns), half),
+            VMEM_SPACE((2, tail, columns), half),
+            pltpu.SemaphoreType.DMA((4, len(arrays))),
+            pltpu.SemaphoreType.DMA((4, len(arrays))),
+            pltpu.SemaphoreType.DMA((4, len(arrays))),
+            pltpu.SemaphoreType.DMA((3, 2, planes)),
+            pltpu.SemaphoreType.DMA((3, 2, planes)),
+            pltpu.SemaphoreType.DMA((4, planes)),
+            pltpu.SemaphoreType.DMA((4, planes)),
+        ],
+        compiler_params=pltpu.CompilerParams(
+            collective_id=identity, has_side_effects=True, vmem_limit_bytes=VMEM_ASK
+        ),
+    )(*views)
+
+
+class Network:
+    def __init__(self, mesh):
+        self.shape = (mesh.shape["dp"], mesh.shape["fsdp"])
+        self.devices = self.shape[0] * self.shape[1]
+        self.kernels = self.shape[1] == 8
+        self.calls = 0
+
+    def identity(self):
+        self.calls += 1
+        return self.calls
+
+    def gather_small(self, blocks):
+        if not self.kernels:
+            return [lax.all_gather(b, AXES) for b in blocks]
+        gathered = small_gather(blocks, self.shape, self.identity())
+        return [g.reshape(self.devices, *g.shape[2:]) for g in gathered]
+
+    def scatter_small(self, blocks):
+        if not self.kernels:
+            return lax.psum_scatter(blocks, AXES, scatter_dimension=0)
+        return small_scatter(
+            blocks.reshape(*self.shape, *blocks.shape[1:]), self.shape, self.identity()
+        )
+
+    def gather(self, shards):
+        if not self.kernels:
+            return [lax.all_gather(s, AXES, axis=0, tiled=True) for s in shards]
+        heights = tuple(s.shape[0] for s in shards)
+        packed = jnp.concatenate(shards, 0) if len(shards) > 1 else shards[0]
+        return big_gather(packed, heights, self.shape, self.identity())
+
+    def scatter(self, partials):
+        if not self.kernels:
+            return [
+                lax.psum_scatter(
+                    p.astype(jnp.float32), AXES, scatter_dimension=0, tiled=True
+                )
+                for p in partials
+            ]
+        total = big_scatter(partials, self.shape, self.identity())
+        out, low = [], 0
+        for p in partials:
+            height = p.shape[0] // self.devices
+            out.append(total[low : low + height])
+            low += height
+        return out
 
 
 def layer_forward(hidden, wide, tall, pieces, allowed):
@@ -230,6 +900,7 @@
 
 
 def local(
+    mesh,
     word_table,
     position_table,
     head_weights,
@@ -257,6 +928,7 @@
     mlm_labels,
     sop_labels,
 ):
+    network = Network(mesh)
     own = lax.axis_index(AXES)
     words = word_table.shape[0]
     slots = mlm_labels.shape[0]
@@ -266,8 +938,10 @@
     facts = jnp.concatenate([token_ids, mlm_labels, seq_lengths])
     padded = -(-facts.shape[0] // 1024) * 1024
     facts = jnp.pad(facts, (0, padded - facts.shape[0])).reshape(-1, 128)
-    (all_facts,) = gather_rows([facts])
+    places_own = to_half(position_table).astype(jnp.float32)
+    all_facts, place = network.gather_small([facts, places_own])
     all_facts = all_facts.reshape(-1, padded)
+    place = place.reshape(-1, E)
     devices = all_facts.shape[0]
     all_ids = all_facts[:, :ROWS].reshape(-1)
     all_labels = all_facts[:, ROWS : ROWS + slots].reshape(-1)
@@ -278,25 +952,20 @@
     scales = (1.0 / mlm_count, 1.0 / sop_count)
 
     word_half = to_half(word_table)
-    wide, tall, head, place = gather_rows(
-        [
-            to_half(layer_wide).T,
-            to_half(layer_tall),
-            to_half(head_weights).T,
-            to_half(position_table),
-        ]
+    wide, tall, head = network.gather(
+        [to_half(layer_wide).T, to_half(layer_tall), to_half(head_weights).T]
     )
 
     offset = own * words
     column = jnp.arange(words, dtype=jnp.int32)
     select = to_half((all_ids - offset)[:, None] == column[None, :])
-    (found,) = scatter_rows([to_half(product(select, word_half))])
+    (found,) = network.scatter([to_half(product(select, word_half))])
     two = seq_lengths[1] > 0
-    place = place[:ROWS].astype(jnp.float32)
+    place = place[:ROWS]
     placed = jnp.concatenate([place[:BUCKET], jnp.where(two, place[:BUCKET], place[BUCKET:])], 0)
     types = pieces["types"].reshape(2, E)
     embedded = (
-        found.astype(jnp.float32)
+        found
         + placed
         + jnp.where(token_kind[:, None] == 0, types[0:1], types[1:2])
     )
@@ -317,13 +986,21 @@
     dense = times_transpose(picked, head[:E]) + pieces["mlm_b"]
     mlm_hat, mlm_inverse = norm_forward(gelu_tanh(dense))
     rows_half = to_half(mlm_hat * pieces["mlm_g"] + pieces["mlm_lb"])
-    (all_rows,) = gather_rows([rows_half])
+    lifted = -(-slots // 16) * 16
+    (all_rows,) = network.gather_small([jnp.pad(rows_half, ((0, lifted - slots), (0, 0)))])
+    all_rows = all_rows[:, :slots].reshape(-1, E)
     logits = times_transpose(all_rows, word_half) + to_half(decoder_bias).astype(jnp.float32)
     onehot = ((all_labels - offset)[:, None] == column[None, :]).astype(jnp.float32)
     own_top = jnp.max(logits, -1)
     own_total = jnp.sum(jnp.exp(logits - own_top[:, None]), -1)
     own_target = jnp.sum(logits * onehot, -1)
-    stats = lax.all_gather(jnp.stack([own_top, own_total, own_target]), AXES)
+    stats = jnp.concatenate([own_top, own_total, own_target])
+    lifted = -(-stats.shape[0] // 1024) * 1024
+    (stats,) = network.gather_small(
+        [jnp.pad(stats, (0, lifted - stats.shape[0])).reshape(-1, 128)]
+    )
+    stats = stats.reshape(devices, lifted)[:, : 3 * devices * slots]
+    stats = stats.reshape(devices, 3, devices * slots)
     top = jnp.max(stats[:, 0], 0)
     total = jnp.sum(stats[:, 1] * jnp.exp(stats[:, 0] - top[None]), 0)
     log_total = jnp.log(total) + top
@@ -333,7 +1010,9 @@
     )
     back_decoder = column_sum(logits_half)
     back_word_head = transpose_times(logits_half, all_rows)
-    (back_rows,) = scatter_rows([product(logits_half, word_half)])
+    back_rows = network.scatter_small(
+        product(logits_half, word_half).reshape(devices, slots, E)
+    )
     back_mlm_g = jnp.sum(back_rows * mlm_hat, 0)
     back_mlm_lb = jnp.sum(back_rows, 0)
     dense_half = to_half(
@@ -381,7 +1060,7 @@
     back_normed = times_transpose(upstream_half, head[E + D :])
     back_proj = transpose_times(normed_half, upstream_half)
     back_embedded = norm_backward(back_normed, pieces["emb_g"], embed_hat, embed_inverse)
-    (all_back,) = gather_rows([to_half(back_embedded)])
+    (all_back,) = network.gather([to_half(back_embedded)])
     back_word = back_word_head + transpose_times(select, all_back)
     places = position_table.shape[0]
     by_device = all_back.reshape(devices, ROWS, E)
@@ -400,15 +1079,15 @@
     inner_all, outer_all = long(back["inner_half"]), long(back["outer_half"])
     back_wide = jnp.concatenate(
         [
-            transpose_times(joint_all, long(kept["hidden_half"])),
-            transpose_times(branch_all, long(kept["mixed"])),
-            transpose_times(inner_all, long(kept["middle_half"])),
+            to_half(transpose_times(joint_all, long(kept["hidden_half"]))),
+            to_half(transpose_times(branch_all, long(kept["mixed"]))),
+            to_half(transpose_times(inner_all, long(kept["middle_half"]))),
         ],
         0,
     )
-    back_tall = transpose_times(long(kept["active"]), outer_all)
-    back_head = jnp.concatenate([back_mlm, back_pool, back_proj], 0)
-    sum_wide, sum_tall, sum_head = scatter_rows([back_wide, back_tall, back_head])
+    back_tall = to_half(transpose_times(long(kept["active"]), outer_all))
+    back_head = to_half(jnp.concatenate([back_mlm, back_pool, back_proj], 0))
+    sum_wide, sum_tall, sum_head = network.scatter([back_wide, back_tall, back_head])
 
     joint_sum = column_sum(joint_all)
     norms = jnp.sum(back["norms"], 0)
@@ -438,8 +1117,17 @@
     )
     shards = (back_word, back_place, sum_head.T, back_decoder, sum_wide.T, sum_tall)
     local_squares = jnp.sum(jnp.stack([jnp.sum(s * s) for s in shards]))
-    reduced, sop_total, squares = lax.psum((vector_grad, sop_sum, local_squares), AXES)
-    grad_norm = jnp.sqrt(squares + jnp.sum(reduced * reduced))
+    total = vector_grad.shape[0]
+    share = -(-total // (devices * 1024)) * 1024
+    own_vector = network.scatter_small(
+        jnp.pad(vector_grad, (0, devices * share - total)).reshape(devices, -1, 128)
+    )
+    scalars = jnp.stack([sop_sum, local_squares])
+    scalars = jnp.pad(scalars, (0, 1024 - scalars.shape[0])).reshape(8, 128)
+    (last,) = network.gather_small([jnp.concatenate([own_vector, scalars], 0)])
+    reduced = last[:, : share // 128].reshape(-1)[:total]
+    sop_total = jnp.sum(last[:, share // 128, 0])
+    grad_norm = jnp.sqrt(jnp.sum(last[:, share // 128, 1]) + jnp.sum(reduced * reduced))
     factor = jnp.minimum(1.0, CLIP_NORM / (grad_norm + NORM_EPSILON))
     updates = []
     for weight, gradient, first, second, rate in (
@@ -461,7 +1149,7 @@
     flat = P(AXES)
     whole = P()
     return jax.shard_map(
-        local,
+        functools.partial(local, mesh),
         mesh=mesh,
         in_specs=(rows, rows, columns, flat, columns, rows, whole)
         + (rows, rows) * 2

time: 1460 us -> 664 us (0.45)
  waiting for transfers between devices: 861 us -> 0 us
  Pallas kernels: 0 us -> 269 us
  blocking collectives: 200 us -> 0 us
    reduce_scatter x4 -> x0, waiting for transfers between devices: 527 us -> none  [scatter_rows(): lax.psum_scatter(s, AXES, scatter_dimension=0, tiled=True)]
    pallas_call x0 -> x10, Pallas kernels: none -> 269 us  [the longest x2 97.4 us: big_scatter(): pl.pallas_call(functools.partial(big_scatter_kernel, planes, rows, tuple(...]
    all_gather x4 -> x0, waiting for transfers between devices: 206 us -> none  [gather_rows(): return [lax.all_gather(s, AXES, axis=0, tiled=True) for s in shards]]
    all_gather x4 -> x0, blocking collectives: 159 us -> none  [the longest x3 121 us: gather_rows(): return [lax.all_gather(s, AXES, axis=0, tiled=True) for s in shards]]
    unnamed x10 -> x0, waiting for transfers between devices: 128 us -> none
    psum x1 -> x0, blocking collectives: 40.1 us -> none  [local(): lax.psum((vector_grad, sop_sum, local_squares), AXES)]
    concatenate x2 -> x4, other arithmetic: 9.35 us -> 24.5 us  [the longest x1 21.8 us: local(): jnp.concatenate([to_half(transpose_times(joint_all, long(kept['hidden_hal...]
  transfers between devices with their start and end apart: 9 -> 0, of which waited for: 9 -> 0; matrix products, arithmetic and copies ran while one was open for 5% -> 0% of each run, Pallas kernels for 0% -> 0%
where the time goes in v2:
time: 664 us; the launch traced here: 657 us
  Pallas kernels  269 us (41%)
  matrix products  175 us (26%)
  other arithmetic  129 us (19%)
  local copies, waits for them, and re-layouts  70.4 us (11%)
  between operations  12 us (2%)
    pallas_call x2, Pallas kernels, big_scatter(): pl.pallas_call(functools.partial(big_scatter_kernel, planes, rows, tuple(...  97.4 us
    pallas_call x2, Pallas kernels, big_gather(): pl.pallas_call(functools.partial(big_gather_kernel, planes, rows, tuple(m...  92.2 us
    dot_general x20, matrix products, times_transpose(): lax.dot_general(a, b, (((1,), (1,)), ((), ())), preferred_element_type=jn...  67.2 us
    pallas_call x4, Pallas kernels, small_gather(): pl.pallas_call(functools.partial(small_gather_kernel, count, planes, widt...  52.4 us
    dot_general x22, matrix products, product(): return jnp.dot(a, b, preferred_element_type=jnp.float32)  49 us
    dot_general x9, matrix products, transpose_times(): lax.dot_general(a, b, (((0,), (0,)), ((), ())), preferred_element_type=jn...  29 us
    dynamic_update_slice x20, other arithmetic, local(): lax.scan(lambda h, unused: layer_forward(h, wide, tall, pieces, allowed),...  27.8 us
    pallas_call x2, Pallas kernels, small_scatter(): pl.pallas_call(functools.partial(small_scatter_kernel, planes, width), ou...  27.2 us

profile of v2, /device:TPU:0, one launch (start us, length us, event | category | flops | bytes accessed | tf_op | source)
XLA Modules:
  0.0 656.7 jit_solution(1028242155122958137)
XLA Ops:
  6.6 15.5 %shard_map.449 = (s32[4,8,8,128]{3,2,1,0:T(8,128)}, f32[4,8,16,128]{3,2,1,0:T(8,128)}) custom-call(s32[8,128]{1,0:T(8,128)} %pad_bitcast_fusion.refs_0_, f32[16,128]{1,0:T(8,128)} %convert_convert_fusion.refs_1_), custom_call_target="tpu_custom_call" | custom-call | tf_op jit(solution)/shard_map/pallas_call | solution.py:215
  24.0 11.2 %fusion.76 = bf16[8192,128]{1,0:T(8,128)(2,1)} fusion(s32[8192]{0:T(1024)S(1)} %bitcast.372, f32[960,128]{1,0:T(8,128)} %param.30), kind=kOutput, calls=%fused_computation.132 | convolution fusion | flops 2022301696 | bytes 2621440 | tf_op jit(solution)/shard_map/dot_general | solution.py:76
  35.2 23.9 %shard_map.450 = f32[256,128]{1,0:T(8,128)} custom-call(bf16[4,4,2,256,128]{4,3,2,1,0:T(8,128)(2,1)} %bitcast.357), custom_call_target="tpu_custom_call" | custom-call | tf_op jit(solution)/shard_map/pallas_call | solution.py:731
  61.4 67.6 %shard_map.451 = (bf16[4,4,2,192,768]{4,3,2,1,0:T(8,128)(2,1)}, bf16[4,4,2,96,768]{4,3,2,1,0:T(8,128)(2,1)}, bf16[4,4,2,32,768]{4,3,2,1,0:T(8,128)(2,1)}) custom-call(bf16[320,768]{1,0:T(8,128)(2,1)} %pad_maximum_fusion.3.x), custom_call_target="tpu_custom_call" | custom-call | tf_op jit(solution)/shard_map/pallas_call | solution.py:467
  138.1 94.9 %while.58 = (s32[]{:T(128)}, f32[256,768]{1,0:T(8,128)S(1)}, bf16[4,256,3072]{2,1,0:T(8,128)(2,1)}, f32[4,256,768]{2,1,0:T(8,128)}, f32[4,256,768]{2,1,0:T(8,128...) while((s32[]{:T(128)}, f32[256,768]{1,0:T(8,128)S(1)}, ...), condition=%wide.region_9.10_spmd.clone, body=%wide.region_2.0_spmd.clone.sunk | while | flops 3855815936 | bytes 110778992 | solution.py:976
  161.7 4.2 bitcast_dynamic-update-slice_fusion.23
  185.4 4.1 bitcast_dynamic-update-slice_fusion.23
  235.5 11.7 %shard_map.452 = bf16[4,8,48,128]{3,2,1,0:T(8,128)(2,1)} custom-call(bf16[48,128]{1,0:T(8,128)(2,1)} %pad.25.refs_0_), custom_call_target="tpu_custom_call" | custom-call | tf_op jit(solution)/shard_map/pallas_call | solution.py:215
  256.3 14.2 %shard_map.453 = f32[4,8,32,128]{3,2,1,0:T(8,128)} custom-call(f32[32,128]{1,0:T(8,128)} %fusion.114.refs_0_), custom_call_target="tpu_custom_call" | custom-call | tf_op jit(solution)/shard_map/pallas_call | solution.py:215
  274.2 4.6 convert_reduce_fusion.2
  282.0 15.9 %shard_map.454 = f32[40,128]{1,0:T(8,128)} custom-call(f32[4,8,40,128]{3,2,1,0:T(8,128)} %bitcast.354), custom_call_target="tpu_custom_call" | custom-call | tf_op jit(solution)/shard_map/pallas_call | solution.py:269
  315.3 126.8 %while.57 = (s32[]{:T(128)}, f32[256,768]{1,0:T(8,128)S(1)}, bf16[4,256,768]{2,1,0:T(8,128)(2,1)S(1)}, bf16[4,256,3072]{2,1,0:T(8,128)(2,1)}, bf16[4,256,2304]{1...) while((s32[]{:T(128)}, f32[256,768]{1,0:T(8,128)S(1)}, ...), condition=%wide.region_35.36_spmd, body=%wide.region_25.35_spmd.sunk | while | flops 4053470208 | bytes 122044864 | solution.py:1055
  320.2 7.5 %bitcast_dynamic-update-slice_fusion.21 = (bf16[4,256,3072]{2,1,0:T(8,128)(2,1)}, bf16[256,3072]{1,0:T(8,128)(2,1)S(1)}) fusion(bf16[4,256,3072]{2,1,0:T(8,128)(2,1)} %get-tuple-element.1516, s32[]{:T(128)S(6)} %sub.514, f32[4,256,3072]{2,1,0:T(8,128)} %get-tuple-element.1546, bf16[3072,768]{1,0:T(8,128)(2,1)} %get-tuple-element.1545, ...), kind=kOutput, calls=%fused_computation.24.clone.1 | convolution fusion | flops 1223098368 | bytes 11796484 | tf_op jit(solution)/shard_map/while/body/eval_jaxpr/dot_general | solution.py:80
  351.7 7.4 %bitcast_dynamic-update-slice_fusion.21 = (bf16[4,256,3072]{2,1,0:T(8,128)(2,1)}, bf16[256,3072]{1,0:T(8,128)(2,1)S(1)}) fusion(bf16[4,256,3072]{2,1,0:T(8,128)(2,1)} %get-tuple-element.1516, s32[]{:T(128)S(6)} %sub.514, f32[4,256,3072]{2,1,0:T(8,128)} %get-tuple-element.1546, bf16[3072,768]{1,0:T(8,128)(2,1)} %get-tuple-element.1545, ...), kind=kOutput, calls=%fused_computation.24.clone.1 | convolution fusion | flops 1223098368 | bytes 11796484 | tf_op jit(solution)/shard_map/while/body/eval_jaxpr/dot_general | solution.py:80
  383.2 7.5 %bitcast_dynamic-update-slice_fusion.21 = (bf16[4,256,3072]{2,1,0:T(8,128)(2,1)}, bf16[256,3072]{1,0:T(8,128)(2,1)S(1)}) fusion(bf16[4,256,3072]{2,1,0:T(8,128)(2,1)} %get-tuple-element.1516, s32[]{:T(128)S(6)} %sub.514, f32[4,256,3072]{2,1,0:T(8,128)} %get-tuple-element.1546, bf16[3072,768]{1,0:T(8,128)(2,1)} %get-tuple-element.1545, ...), kind=kOutput, calls=%fused_computation.24.clone.1 | convolution fusion | flops 1223098368 | bytes 11796484 | tf_op jit(solution)/shard_map/while/body/eval_jaxpr/dot_general | solution.py:80
  414.9 7.5 %bitcast_dynamic-update-slice_fusion.21 = (bf16[4,256,3072]{2,1,0:T(8,128)(2,1)}, bf16[256,3072]{1,0:T(8,128)(2,1)S(1)}) fusion(bf16[4,256,3072]{2,1,0:T(8,128)(2,1)} %get-tuple-element.1516, s32[]{:T(128)S(6)} %sub.514, f32[4,256,3072]{2,1,0:T(8,128)} %get-tuple-element.1546, bf16[3072,768]{1,0:T(8,128)(2,1)} %get-tuple-element.1545, ...), kind=kOutput, calls=%fused_computation.24.clone.1 | convolution fusion | flops 1223098368 | bytes 11796484 | tf_op jit(solution)/shard_map/while/body/eval_jaxpr/dot_general | solution.py:80
  454.6 11.3 %shard_map.455 = f32[8,128]{1,0:T(8,128)} custom-call(f32[4,8,8,128]{3,2,1,0:T(8,128)} %bitcast.363), custom_call_target="tpu_custom_call" | custom-call | tf_op jit(solution)/shard_map/pallas_call | solution.py:269
  469.0 10.0 %bitcast_convert_fusion.4 = bf16[3072,768]{1,0:T(8,128)(2,1)} fusion(bf16[4,256,3072]{2,1,0:T(8,128)(2,1)} %get-tuple-element.546, bf16[4,256,768]{2,1,0:T(8,128)(2,1)} %get-tuple-element.541), kind=kOutput, calls=%fused_computation.134 | convolution fusion | flops 4834197504 | bytes 12582912 | tf_op jit(solution)/shard_map/dot_general | solution.py:84
  484.6 5.5 bitcast_convert_fusion.5
  490.1 21.8 %pad_maximum_fusion.1 = bf16[6144,768]{1,0:T(8,128)(2,1)} fusion(bf16[3072,768]{1,0:T(8,128)(2,1)S(1)} %bitcast_convert_fusion.5, bf16[768,768]{1,0:T(8,128)(2,1)S(1)} %bitcast_convert_fusion.7, bf16[2304,768]{1,0:T(8,128)(2,1)S(1)} %bitcast_convert_fusion.6), kind=kLoop, calls=%fused_computation.133 | loop fusion | flops 28311552 | bytes 18874368 | tf_op jit(solution)/shard_map/concatenate | solution.py:1080
  511.9 73.5 %shard_map.457 = f32[320,768]{1,0:T(8,128)} custom-call(bf16[4,4,2,192,768]{4,3,2,1,0:T(8,128)(2,1)} %bitcast.334, bf16[4,4,2,96,768]{4,3,2,1,0:T(8,128)(2,1)} %bitcast.353, bf16[4,4,2,32,768]{4,3,2,1,0:T(8,128)(2,1)} %bitcast.346), custom_call_target="tpu_custom_call" | custom-call | tf_op jit(solution)/shard_map/pallas_call | solution.py:731
  587.1 24.6 %shard_map.456 = bf16[4,4,2,256,128]{4,3,2,1,0:T(8,128)(2,1)} custom-call(bf16[256,128]{1,0:T(8,128)(2,1)} %get-tuple-element.978.x), custom_call_target="tpu_custom_call" | custom-call | tf_op jit(solution)/shard_map/pallas_call | solution.py:467
  615.5 6.1 multiply_reduce_fusion.5
  629.0 11.1 %shard_map.458 = f32[4,8,16,128]{3,2,1,0:T(8,128)} custom-call(f32[16,128]{1,0:T(8,128)} %pad_maximum_fusion.4.refs_0_), custom_call_target="tpu_custom_call" | custom-call | tf_op jit(solution)/shard_map/pallas_call | solution.py:215
  (620 shorter events, 276.4 us)
Async XLA Ops:
  3.9 55.2 %copy-start.65 = (pred[256]{0:T(512)(128)(4,1)}, pred[256]{0:T(512)(128)(4,1)S(1)}, u32[]{:S(2)}) copy-start(pred[256]{0:T(512)(128)(4,1)S(1)} %get-tuple-element.1053) | copy-start | bytes 772
  24.0 35.1 %copy-start.27 = (f32[13184]{0:T(1024)S(1)}, f32[13184]{0:T(1024)}, u32[]{:S(2)}) copy-start(f32[13184]{0:T(1024)} %param.36) | copy-start | bytes 158212
  35.2 25.3 %copy-start.14 = (f32[768,192]{0,1:T(8,128)S(1)}, f32[768,192]{0,1:T(8,128)}, u32[]{:S(2)}) copy-start(f32[768,192]{0,1:T(8,128)} %param.34) | copy-start | bytes 1769476
  35.2 25.4 %copy-start.18 = (f32[96,768]{1,0:T(8,128)S(1)}, f32[96,768]{1,0:T(8,128)}, u32[]{:S(2)}) copy-start(f32[96,768]{1,0:T(8,128)} %param.35) | copy-start | bytes 884740
  35.2 25.4 %copy-start.25 = (f32[768,32]{0,1:T(8,128)S(1)}, f32[768,32]{0,1:T(8,128)}, u32[]{:S(2)}) copy-start(f32[768,32]{0,1:T(8,128)} %param.32) | copy-start | bytes 294916
  59.1 76.4 %copy-start.57 = (f32[128]{0:T(128)}, f32[128]{0:T(128)S(1)}, u32[]{:S(2)}) copy-start(f32[128]{0:T(128)S(1)} %get-tuple-element.1037) | copy-start | bytes 1540
  59.2 76.4 %copy-start.63 = (f32[128]{0:T(128)}, f32[128]{0:T(128)S(1)}, u32[]{:S(2)}) copy-start(f32[128]{0:T(128)S(1)} %get-tuple-element.1036) | copy-start | bytes 1540
  60.3 68.8 %copy-start.8 = (f32[256,128]{1,0:T(8,128)}, f32[256,128]{1,0:T(8,128)S(1)}, u32[]{:S(2)}) copy-start(f32[256,128]{1,0:T(8,128)S(1)} %get-tuple-element.989) | copy-start | bytes 393220
  60.3 75.3 %copy-start.39 = (f32[256]{0:T(256)}, f32[256]{0:T(256)S(1)}, u32[]{:S(2)}) copy-start(f32[256]{0:T(256)S(1)} %broadcast_multiply_fusion.8) | copy-start | bytes 3076
  60.5 75.1 %copy-start.50 = (f32[256]{0:T(256)}, f32[256]{0:T(256)S(1)}, u32[]{:S(2)}) copy-start(f32[256]{0:T(256)S(1)} %add_rsqrt_fusion.2) | copy-start | bytes 3076
  138.1 95.0 %copy-start.79 = (s32[40]{0:T(128)S(1)}, s32[40]{0:T(128)}, u32[]{:S(2)}) copy-start(s32[40]{0:T(128)} %param.53) | copy-start | bytes 484
  138.1 110.1 %copy-start.53 = (f32[960]{0:T(1024)S(1)}, f32[960]{0:T(1024)}, u32[]{:S(2)}) copy-start(f32[960]{0:T(1024)} %param.33) | copy-start | bytes 11524
  278.8 21.8 %copy-start.6 = (bf16[4,4,2,32,768]{4,3,2,1,0:T(8,128)(2,1)S(1)}, bf16[4,4,2,32,768]{4,3,2,1,0:T(8,128)(2,1)}, u32[]{:S(2)}) copy-start(bf16[4,4,2,32,768]{4,3,2,1,0:T(8,128)(2,1)} %get-tuple-element.526) | copy-start | bytes 4718596
  280.3 21.6 %copy-start.28 = (f32[13184]{0:T(1024)S(1)}, f32[13184]{0:T(1024)}, u32[]{:S(2)}) copy-start(f32[13184]{0:T(1024)} %param.36) | copy-start | bytes 158212
  280.3 21.8 %copy-start.75 = (s32[2]{0:T(128)S(1)}, s32[2]{0:T(128)}, u32[]{:S(2)}) copy-start(s32[2]{0:T(128)} %param.55) | copy-start | bytes 28
  447.7 19.1 %copy-start.45 = (bf16[1,768]{1,0:T(2,128)(2,1)S(1)}, bf16[1,768]{1,0:T(2,128)(2,1)}, u32[]{:S(2)}) copy-start(bf16[1,768]{1,0:T(2,128)(2,1)} %copy-done.44) | copy-start | bytes 4612
  447.7 19.1 %copy-start.47 = (bf16[1,768]{1,0:T(2,128)(2,1)S(1)}, bf16[1,768]{1,0:T(2,128)(2,1)}, u32[]{:S(2)}) copy-start(bf16[1,768]{1,0:T(2,128)(2,1)} %copy-done.46) | copy-start | bytes 4612
  511.9 99.8 %copy-start.73 = (pred[32,1]{0,1:T(4,128)(4,1)S(1)}, pred[32,1]{0,1:T(4,128)(4,1)}, u32[]{:S(2)}) copy-start(pred[32,1]{0,1:T(4,128)(4,1)} %copy-done.72) | copy-start | bytes 100
  585.4 29.1 %copy-start.1 = (bf16[1280,960]{0,1:T(8,128)(2,1)S(1)}, bf16[1280,960]{0,1:T(8,128)(2,1)}, u32[]{:S(2)}) copy-start(bf16[1280,960]{0,1:T(8,128)(2,1)} %copy-done) | copy-start | bytes 7372804
  585.5 29.1 %copy-start.13 = (bf16[32,40,128]{2,1,0:T(8,128)(2,1)S(1)}, bf16[32,40,128]{2,1,0:T(8,128)(2,1)}, u32[]{:S(2)}) copy-start(bf16[32,40,128]{2,1,0:T(8,128)(2,1)} %copy-done.12) | copy-start | bytes 983044
  615.5 31.5 %copy-start.19 = (f32[96,768]{1,0:T(8,128)S(1)}, f32[96,768]{1,0:T(8,128)}, u32[]{:S(2)}) copy-start(f32[96,768]{1,0:T(8,128)} %param.35) | copy-start | bytes 884740
  621.6 27.7 %copy-start.15 = (f32[768,192]{0,1:T(8,128)S(1)}, f32[768,192]{0,1:T(8,128)}, u32[]{:S(2)}) copy-start(f32[768,192]{0,1:T(8,128)} %param.34) | copy-start | bytes 1769476
  621.6 27.7 %copy-start.20 = (f32[768,192]{0,1:T(8,128)S(1)}, f32[768,192]{0,1:T(8,128)}, u32[]{:S(2)}) copy-start(f32[768,192]{0,1:T(8,128)} %param.45) | copy-start | bytes 1769476
  621.6 27.7 %copy-start.21 = (f32[768,192]{0,1:T(8,128)S(1)}, f32[768,192]{0,1:T(8,128)}, u32[]{:S(2)}) copy-start(f32[768,192]{0,1:T(8,128)} %param.46) | copy-start | bytes 1769476
  (109 other events, 661.9 us)

commit v3 on v2

--- a/solution.py
+++ b/solution.py
@@ -65,7 +65,9 @@
 
 
 def join_vectors(gradients):
-    return jnp.concatenate([gradients[member].reshape(-1) for member, length in layout()])
+    order = ("proj_b", "layer", "pool_b", "cls", "ff_b", "emb_g", "emb_b")
+    order = order + ("mlm_b", "mlm_g", "mlm_lb", "types")
+    return jnp.concatenate([gradients[member].reshape(-1) for member in order])
 
 
 def to_half(x):
@@ -118,16 +120,14 @@
     )
 
 
-def row_layout(lengths):
+def row_kind(lengths):
     row_index = jnp.arange(ROWS, dtype=jnp.int32)
     second = (row_index >= BUCKET) & (lengths[1] > 0)
     seq_id = second.astype(jnp.int32)
     position = row_index - BUCKET * seq_id
     own_length = jnp.where(second, lengths[1], lengths[0])
-    is_live = position < own_length
     token_kind = (position >= own_length // 2).astype(jnp.int32)
-    allowed = (seq_id[:, None] == seq_id[None, :]) & is_live[None, :]
-    return (token_kind, allowed)
+    return token_kind
 
 
 MESH_ID = pl.DeviceIdType.MESH
@@ -756,6 +756,437 @@
     )(*views)
 
 
+def far_first(i, z, planes):
+    low = (2 * z < planes).astype(jnp.int32)
+    falling = planes - 1 - i - (i >= planes - 1 - z).astype(jnp.int32)
+    rising = i + (i >= z).astype(jnp.int32)
+    last = (jnp.int32(i) == planes - 1).astype(jnp.int32)
+    return last * z + (1 - last) * (low * falling + (1 - low) * rising)
+
+
+def finish_kernel(
+    planes,
+    heights,
+    split,
+    left_wide,
+    left_tall,
+    rights,
+    outer,
+    head_grad,
+    own_rows,
+    vector_terms,
+    out,
+    all_rows,
+    own_vector,
+    both,
+    side,
+    half_in,
+    full_in,
+    line_in,
+    tail_line,
+    tail_half,
+    tail_full,
+    wide_buf,
+    tall_buf,
+    vector_in,
+    vector_mid,
+    vector_last,
+    fetch,
+    head_load,
+    side_send,
+    side_recv,
+    send,
+    recv,
+    tail_send,
+    tail_recv,
+    row_send,
+    row_recv,
+    vec_send,
+    vec_recv,
+):
+    width = 8
+    wide_height, tall_height, head_height = heights
+    rows = wide_height + tall_height + head_height
+    z, c, cols = places()
+    q = cols[0]
+    f = q * 2 + c
+    x, y = lax.rem(q, 2), q // 2
+    cuts = cuts_of(rows)
+    head, tail = cuts
+    head_rows, tail_rows = head[1] - head[0], tail[1] - tail[0]
+    at_x, at_y, mate = (z, cols[1] * 2 + c), (z, cols[2] * 2 + c), (z, q * 2 + 1 - c)
+    above, below = z < planes - 1, z > 0
+    up, down = (z + 1, f), (z - 1, f)
+    line = [(lax.rem(z + d, planes), f) for d in range(1, planes)]
+    plane = [(z, lax.rem(f + d, width)) for d in range(1, width)]
+    greet([(None, who) for who in line + plane])
+    order = (DIAGONAL, ACROSS_X, ACROSS_Y, OWN)
+    sent = []
+
+    def push(condition, make):
+        maybe(condition, lambda: make().start())
+        sent.append((condition, make))
+
+    def piece(ref, span):
+        return ref.at[pl.ds(span[0], span[1] - span[0])]
+
+    def plane_at(i):
+        return far_first(i, z, planes)
+
+    def chip_of(n):
+        place, i = n // planes, lax.rem(n, planes)
+        flip_x, flip_y = 1 - place // 2, 1 - lax.rem(place, 2)
+        return plane_at(i) * 4 + 2 * lax.rem(y + flip_y, 2) + lax.rem(x + flip_x, 2)
+
+    def fetches(n):
+        k, slot = chip_of(n), lax.rem(n, 2)
+        wide_rows = pl.ds(pl.multiple_of(k * 2 * wide_height, 16), 2 * wide_height)
+        tall_rows = pl.ds(pl.multiple_of(k * 2 * tall_height, 16), 2 * tall_height)
+        return (
+            pltpu.make_async_copy(
+                left_wide.at[wide_rows], wide_buf.at[slot], fetch.at[0, slot]
+            ),
+            pltpu.make_async_copy(
+                left_tall.at[tall_rows], tall_buf.at[slot], fetch.at[1, slot]
+            ),
+        )
+
+    for copy in fetches(jnp.int32(0)):
+        copy.start()
+
+    def vector_first(d, who):
+        return remote(
+            vector_terms.at[:, who[1]], vector_in.at[d], vec_send.at[0, d], vec_recv.at[0, d], who
+        )
+
+    def vector_second(d, who):
+        return remote(
+            vector_mid.at[who[0]], vector_last.at[d], vec_send.at[1, d], vec_recv.at[1, d], who
+        )
+
+    def row_line(d, who):
+        return remote(
+            own_rows, all_rows.at[z, q, c], row_send.at[0, d], row_recv.at[0, d], who
+        )
+
+    def row_plane(col):
+        return remote(
+            all_rows.at[:, q, c],
+            all_rows.at[:, q, c],
+            row_send.at[1, col],
+            row_recv.at[1, col],
+            (z, cols[col] * 2 + c),
+        )
+
+    def row_mate():
+        return remote(
+            all_rows.at[:, :, c], all_rows.at[:, :, c], row_send.at[2, 0], row_recv.at[2, 0], mate
+        )
+
+    for d, who in enumerate(line):
+        push(None, functools.partial(row_line, d, who))
+    for d, who in enumerate(plane):
+        push(None, functools.partial(vector_first, d, who))
+    all_rows[z, q, c] = own_rows[...]
+    head_copies = []
+    for col in order:
+        copy = pltpu.make_async_copy(
+            head_grad.at[:, cols[col]],
+            both.at[:, col, :, pl.ds(wide_height + tall_height, head_height)],
+            head_load.at[col],
+        )
+        copy.start()
+        head_copies.append(copy)
+
+    def side_message(zt, col):
+        return remote(
+            both.at[zt, col, 1 - c],
+            side.at[zt, col],
+            side_send.at[col, zt],
+            side_recv.at[col, zt],
+            mate,
+        )
+
+    def half_message(zt, which):
+        return remote(
+            piece(both.at[zt, DIAGONAL, c], half_of(head, which)),
+            half_in.at[which, zt],
+            send.at[0, which, zt],
+            recv.at[0, which, zt],
+            (at_x, at_y)[which],
+        )
+
+    def full_message(zt, which):
+        return remote(
+            piece(both.at[zt, (ACROSS_X, ACROSS_Y)[which], c], head),
+            full_in.at[which, zt],
+            send.at[1, which, zt],
+            recv.at[1, which, zt],
+            (at_x, at_y)[which],
+        )
+
+    def line_message(zt, way):
+        return remote(
+            piece(both.at[zt, OWN, c], head),
+            line_in.at[way, zt],
+            send.at[2, way, zt],
+            recv.at[2, way, zt],
+            (up, down)[way],
+        )
+
+    def tail_message(zt, way):
+        return remote(
+            both.at[zt, :, c, pl.ds(tail[0], tail_rows)],
+            tail_line.at[way, zt],
+            tail_send.at[way, zt],
+            tail_recv.at[way, zt],
+            (up, down)[way],
+        )
+
+    def merged(zt, col):
+        side_message(zt, col).wait_recv()
+        mine = both.at[zt, col, c]
+        accumulate(mine, [mine, side.at[zt, col]], rows)
+        if col == DIAGONAL:
+            half_message(zt, 0).start()
+            half_message(zt, 1).start()
+        elif col != OWN:
+            which = 0 if col == ACROSS_X else 1
+            half_message(zt, 1 - which).wait_recv()
+            target = piece(mine, half_of(head, 1 - which))
+            accumulate(target, [target, half_in.at[1 - which, zt]], head_rows // 2)
+            full_message(zt, which).start()
+
+    for place, col in enumerate(order):
+        head_copies[place].wait()
+
+        def body(i, unused, place=place, col=col):
+            n = place * planes + i
+            for copy in fetches(n):
+                copy.wait()
+
+            @pl.when(n + 1 < 4 * planes)
+            def _():
+                for copy in fetches(n + 1):
+                    copy.start()
+
+            zt, k, slot = plane_at(i), chip_of(n), lax.rem(n, 2)
+            region = (k >= split[0]).astype(jnp.int32) + (k >= split[1]).astype(jnp.int32)
+            product_wide = to_half(nn(wide_buf[slot], rights[region]))
+            both[zt, col, 0, :wide_height] = product_wide[:wide_height]
+            both[zt, col, 1, :wide_height] = product_wide[wide_height:]
+            product_tall = to_half(nn(tall_buf[slot], outer[...]))
+            here = slice(wide_height, wide_height + tall_height)
+            both[zt, col, 0, here] = product_tall[:tall_height]
+            both[zt, col, 1, here] = product_tall[tall_height:]
+            side_message(zt, col).start()
+
+            @pl.when(i > 0)
+            def _():
+                merged(plane_at(i - 1), col)
+
+            return unused
+
+        lax.fori_loop(0, planes, body, 0)
+        merged(z, col)
+        if place == 0:
+            for d, who in enumerate(line):
+                row_line(d, who).wait_recv()
+            for step in (ACROSS_X, ACROSS_Y, DIAGONAL):
+                push(None, functools.partial(row_plane, step))
+            total = vector_terms[:, f]
+            for d, who in enumerate(plane):
+                vector_first(d, who).wait_recv()
+                total = total + vector_in[d]
+            vector_mid[...] = total
+            for d, who in enumerate(line):
+                push(None, functools.partial(vector_second, d, who))
+        elif place == 2:
+            for step in (ACROSS_X, ACROSS_Y, DIAGONAL):
+                remote(
+                    all_rows.at[:, cols[step], c],
+                    all_rows.at[:, cols[step], c],
+                    row_send.at[1, step],
+                    row_recv.at[1, step],
+                    mate,
+                ).wait_recv()
+            push(None, row_mate)
+
+    targets = [plane_at(i) for i in range(planes)]
+
+    def tail_add(zt, way):
+        tail_message(zt, way).wait_recv()
+        for col in range(4):
+            target = piece(both.at[zt, col, c], tail)
+            accumulate(target, [target, tail_line.at[way, zt, col]], tail_rows)
+
+    def tail_step(zt):
+        for way, valid in ((0, zt > z), (1, zt < z)):
+            behind = (below, above)[way]
+            pl.when(jnp.logical_and(valid, behind))(lambda way=way: tail_add(zt, way))
+            push(valid, functools.partial(tail_message, zt, way))
+
+    def third(zt):
+        for which in (0, 1):
+            full_message(zt, which).wait_recv()
+        base = [piece(both.at[zt, OWN, c], head), full_in.at[0, zt], full_in.at[1, zt]]
+        accumulate(base[0], base, head_rows)
+        for way, valid in ((0, zt > z), (1, zt < z)):
+            behind = (below, above)[way]
+
+            def add(way=way):
+                line_message(zt, way).wait_recv()
+                accumulate(base[0], [base[0], line_in.at[way, zt]], head_rows)
+
+            pl.when(jnp.logical_and(valid, behind))(add)
+            push(valid, functools.partial(line_message, zt, way))
+
+    def tail_half_message(which):
+        return remote(
+            piece(both.at[z, DIAGONAL, c], half_of(tail, which)),
+            tail_half.at[which],
+            tail_send.at[2, which],
+            tail_recv.at[2, which],
+            (at_x, at_y)[which],
+        )
+
+    def tail_full_message(which):
+        return remote(
+            piece(both.at[z, (ACROSS_X, ACROSS_Y)[which], c], tail),
+            tail_full.at[which],
+            tail_send.at[3, which],
+            tail_recv.at[3, which],
+            (at_x, at_y)[which],
+        )
+
+    tail_step(targets[0])
+    for number in range(planes - 1):
+        third(targets[number])
+        if number + 1 < planes - 1:
+            tail_step(targets[number + 1])
+    pl.when(below)(lambda: tail_add(z, 0))
+    pl.when(above)(lambda: tail_add(z, 1))
+    for which in (0, 1):
+        push(None, functools.partial(tail_half_message, which))
+    for which, col in ((1, ACROSS_X), (0, ACROSS_Y)):
+        tail_half_message(which).wait_recv()
+        target = piece(both.at[z, col, c], half_of(tail, which))
+        accumulate(target, [target, tail_half.at[which]], tail_rows // 2)
+    for which in (0, 1):
+        push(None, functools.partial(tail_full_message, which))
+    for which in (0, 1):
+        full_message(z, which).wait_recv()
+    goal = piece(out, head)
+    accumulate(
+        goal, [piece(both.at[z, OWN, c], head), full_in.at[0, z], full_in.at[1, z]], head_rows
+    )
+    for present, way in ((below, 0), (above, 1)):
+
+        def add(way=way):
+            line_message(z, way).wait_recv()
+            accumulate(goal, [goal, line_in.at[way, z]], head_rows)
+
+        pl.when(present)(add)
+    for which in (0, 1):
+        tail_full_message(which).wait_recv()
+    accumulate(
+        piece(out, tail),
+        [piece(both.at[z, OWN, c], tail), tail_full.at[0], tail_full.at[1]],
+        tail_rows,
+    )
+    total = vector_mid[z]
+    for d, who in enumerate(line):
+        vector_second(d, who).wait_recv()
+        total = total + vector_last[d]
+    own_vector[...] = total
+    remote(
+        all_rows.at[:, :, 1 - c],
+        all_rows.at[:, :, 1 - c],
+        row_send.at[2, 0],
+        row_recv.at[2, 0],
+        mate,
+    ).wait_recv()
+    for condition, make in sent:
+        maybe(condition, lambda make=make: make().wait_send())
+    for zt in targets:
+        for col in order:
+            side_message(zt, col).wait_send()
+        for which in (0, 1):
+            half_message(zt, which).wait_send()
+            full_message(zt, which).wait_send()
+
+
+def run_finish(
+    left_wide, left_tall, rights, outer, head_grad, own_rows, vector_terms, mesh_shape, identity
+):
+    planes, width = mesh_shape
+    devices = planes * width
+    columns = outer.shape[1]
+    heights = (
+        left_wide.shape[0] // devices,
+        left_tall.shape[0] // devices,
+        head_grad.shape[0] // devices,
+    )
+    rows = sum(heights)
+    long = left_wide.shape[1]
+    split = (3 * D // (2 * heights[0]), 4 * D // (2 * heights[0]))
+    head, tail = (high - low for low, high in cuts_of(rows))
+    half, single = jnp.bfloat16, jnp.float32
+    block = vector_terms.shape[1:]
+    vmem = pl.BlockSpec(memory_space=VMEM_SPACE)
+    any_space = pl.BlockSpec(memory_space=pl.ANY)
+    dma = pltpu.SemaphoreType.DMA
+    out, all_rows, own_vector = pl.pallas_call(
+        functools.partial(finish_kernel, planes, heights, split),
+        out_shape=[
+            jax.ShapeDtypeStruct((rows, columns), single),
+            jax.ShapeDtypeStruct((planes, width // 2, 2, *own_rows.shape), half),
+            jax.ShapeDtypeStruct(block, single),
+        ],
+        in_specs=[any_space, any_space, vmem, vmem, any_space, vmem, vmem],
+        out_specs=[vmem] * 3,
+        scratch_shapes=[
+            VMEM_SPACE((planes, 4, 2, rows, columns), half),
+            VMEM_SPACE((planes, 4, rows, columns), half),
+            VMEM_SPACE((2, planes, head // 2, columns), half),
+            VMEM_SPACE((2, planes, head, columns), half),
+            VMEM_SPACE((2, planes, head, columns), half),
+            VMEM_SPACE((2, planes, 4, tail, columns), half),
+            VMEM_SPACE((2, tail // 2, columns), half),
+            VMEM_SPACE((2, tail, columns), half),
+            VMEM_SPACE((2, 2 * heights[0], long), half),
+            VMEM_SPACE((2, 2 * heights[1], long), half),
+            VMEM_SPACE((width - 1, planes, *block), single),
+            VMEM_SPACE((planes, *block), single),
+            VMEM_SPACE((planes - 1, *block), single),
+            dma((2, 2)),
+            dma((4,)),
+            dma((4, planes)),
+            dma((4, planes)),
+            dma((3, 2, planes)),
+            dma((3, 2, planes)),
+            dma((4, planes)),
+            dma((4, planes)),
+            dma((3, 4)),
+            dma((3, 4)),
+            dma((2, width)),
+            dma((2, width)),
+        ],
+        compiler_params=pltpu.CompilerParams(
+            collective_id=identity, has_side_effects=True, vmem_limit_bytes=VMEM_ASK
+        ),
+    )(
+        left_wide,
+        left_tall,
+        rights,
+        outer,
+        head_grad.reshape(planes, width // 2, 2, heights[2], columns),
+        own_rows,
+        vector_terms.reshape(planes, width, *block),
+    )
+    return out, heights, all_rows.reshape(-1, own_rows.shape[1]), own_vector
+
+
 class Network:
     def __init__(self, mesh):
         self.shape = (mesh.shape["dp"], mesh.shape["fsdp"])
@@ -803,89 +1234,361 @@
             low += height
         return out
 
-
-def layer_forward(hidden, wide, tall, pieces, allowed):
-    hidden_half = to_half(hidden)
-    joint_bias = jnp.concatenate([pieces["q_b"], jnp.zeros_like(pieces["q_b"]), pieces["v_b"]])
-    projected = to_half(times_transpose(hidden_half, wide[: 3 * D]) + joint_bias)
-    heads = projected.reshape(ROWS, 3, HEADS, HEAD_DIM)
-    queries, key_rows, values = (heads[:, 0], heads[:, 1], heads[:, 2])
-    scores = (
-        jnp.einsum("qhd,khd->hqk", queries, key_rows, preferred_element_type=jnp.float32) * SCALE
-    )
-    scores = jnp.where(allowed[None], scores, MASKED)
-    powers = jnp.exp(scores - jnp.max(scores, -1, keepdims=True))
-    weighting = powers / jnp.sum(powers, -1, keepdims=True)
-    mixed = jnp.einsum(
-        "hqk,khd->qhd", to_half(weighting), values, preferred_element_type=jnp.float32
-    )
-    mixed = to_half(mixed.reshape(ROWS, D))
-    first_sum = hidden + times_transpose(mixed, wide[3 * D : 4 * D]) + pieces["o_b"]
-    hat_one, inverse_one = norm_forward(first_sum)
-    middle = hat_one * pieces["ln1_g"] + pieces["ln1_b"]
-    middle_half = to_half(middle)
-    inner = times_transpose(middle_half, wide[4 * D :]) + pieces["ff_b"]
-    active = to_half(gelu_tanh(inner))
-    second_sum = middle + product(active, tall) + pieces["ffo_b"]
-    hat_two, inverse_two = norm_forward(second_sum)
-    output = hat_two * pieces["ln2_g"] + pieces["ln2_b"]
-    kept = {
-        "hidden_half": hidden_half,
-        "projected": projected,
-        "weighting": weighting,
-        "mixed": mixed,
-        "hat_one": hat_one,
-        "inverse_one": inverse_one,
-        "middle_half": middle_half,
-        "inner": inner,
-        "active": active,
-        "hat_two": hat_two,
-        "inverse_two": inverse_two,
-    }
-    return (output, kept)
-
-
-def layer_backward(upstream, kept, wide, tall, pieces):
-    gain_two = jnp.sum(upstream * kept["hat_two"], 0)
-    shift_two = jnp.sum(upstream, 0)
-    back_second = norm_backward(upstream, pieces["ln2_g"], kept["hat_two"], kept["inverse_two"])
-    outer_half = to_half(back_second)
-    inner_half = to_half(times_transpose(outer_half, tall) * gelu_slope(kept["inner"]))
-    back_middle = back_second + product(inner_half, wide[4 * D :])
-    gain_one = jnp.sum(back_middle * kept["hat_one"], 0)
-    shift_one = jnp.sum(back_middle, 0)
-    back_first = norm_backward(back_middle, pieces["ln1_g"], kept["hat_one"], kept["inverse_one"])
-    branch_half = to_half(back_first)
-    back_mixed = to_half(product(branch_half, wide[3 * D : 4 * D])).reshape(ROWS, HEADS, HEAD_DIM)
-    heads = kept["projected"].reshape(ROWS, 3, HEADS, HEAD_DIM)
-    queries, key_rows, values = (heads[:, 0], heads[:, 1], heads[:, 2])
-    weighting = kept["weighting"]
-    back_soft = jnp.einsum("qhd,khd->hqk", back_mixed, values, preferred_element_type=jnp.float32)
-    scores_half = to_half(
-        weighting * (back_soft - jnp.sum(weighting * back_soft, -1, keepdims=True))
-    )
-    back_queries = (
-        jnp.einsum("hqk,khd->qhd", scores_half, key_rows, preferred_element_type=jnp.float32)
-        * SCALE
-    )
-    back_key_rows = (
-        jnp.einsum("hqk,qhd->khd", scores_half, queries, preferred_element_type=jnp.float32) * SCALE
-    )
-    back_values = jnp.einsum(
-        "hqk,qhd->khd", to_half(weighting), back_mixed, preferred_element_type=jnp.float32
-    )
-    joint_half = to_half(
-        jnp.stack([back_queries, back_key_rows, back_values], 1).reshape(ROWS, 3 * D)
-    )
-    back_hidden = back_first + product(joint_half, wide[: 3 * D])
-    out = {
-        "joint_half": joint_half,
-        "branch_half": branch_half,
-        "inner_half": inner_half,
-        "outer_half": outer_half,
-        "norms": jnp.stack([gain_one, shift_one, gain_two, shift_two]),
-    }
-    return (back_hidden, out)
+    def finish(self, left_wide, left_tall, rights, outer, head_grad, own_rows, vector):
+        total = vector.shape[0]
+        share = -(-total // (self.devices * 1024)) * 1024
+        vector = jnp.pad(vector, (0, self.devices * share - total))
+        vector = vector.reshape(self.devices, -1, 128)
+        if self.kernels:
+            out, heights, all_rows, own_vector = run_finish(
+                left_wide,
+                left_tall,
+                rights,
+                outer,
+                to_half(head_grad),
+                own_rows,
+                vector,
+                self.shape,
+                self.identity(),
+            )
+            first, second = heights[0], heights[0] + heights[1]
+            return out[:first], out[first:second], out[second:], all_rows, own_vector
+        back_wide = jnp.concatenate(
+            [
+                product(left_wide[: 3 * D], rights[0]),
+                product(left_wide[3 * D : 4 * D], rights[1]),
+                product(left_wide[4 * D :], rights[2]),
+            ],
+            0,
+        )
+        sums = self.scatter([back_wide, product(left_tall, outer), head_grad])
+        return (*sums, self.gather([own_rows])[0], self.scatter_small(vector))
+
+
+def nt(a, b):
+    return lax.dot_general(a, b, (((1,), (1,)), ((), ())), preferred_element_type=jnp.float32)
+
+
+def nn(a, b):
+    return jnp.dot(a, b, preferred_element_type=jnp.float32)
+
+
+def tn(a, b):
+    return lax.dot_general(a, b, (((0,), (0,)), ((), ())), preferred_element_type=jnp.float32)
+
+
+CHUNK = 512
+PAIR = 2 * HEAD_DIM
+PROJ_B, Q_B, V_B, O_B, LN1_G, LN1_B, FFO_B, LN2_G, LN2_B, POOL_B = range(10)
+
+
+def allowed_block(lengths):
+    shape = (ROWS, ROWS)
+    row = lax.broadcasted_iota(jnp.int32, shape, 0)
+    col = lax.broadcasted_iota(jnp.int32, shape, 1)
+    two = lengths[1] > 0
+    row_second = jnp.logical_and(row >= BUCKET, two).astype(jnp.int32)
+    col_second = jnp.logical_and(col >= BUCKET, two).astype(jnp.int32)
+    length = jnp.where(col_second == 1, lengths[1], lengths[0])
+    live = col - BUCKET * col_second < length
+    return jnp.logical_and(row_second == col_second, live)
+
+
+def halves(x):
+    lane = lax.broadcasted_iota(jnp.int32, x.shape, 1)
+    zero = jnp.zeros_like(x)
+    return jnp.where(lane < HEAD_DIM, x, zero), jnp.where(lane < HEAD_DIM, zero, x)
+
+
+def forward_kernel(
+    lengths,
+    start,
+    wide,
+    tall,
+    vec,
+    ff_b,
+    final,
+    rights,
+    projected,
+    weighting,
+    hat_one,
+    inverse_one,
+    slope,
+    active,
+    hat_two,
+    inverse_two,
+    hidden,
+):
+    layer = pl.program_id(0)
+
+    @pl.when(layer == 0)
+    def _():
+        hidden[...] = start[...]
+
+    def row(index):
+        return vec[pl.ds(index, 1), :]
+
+    half = to_half(hidden[...])
+    rights[0] = half
+    for part, bias in ((0, Q_B), (1, None), (2, V_B)):
+        for low in range(0, D, 256):
+            here = part * D + low
+            value = nt(half, wide[pl.ds(here, 256), :])
+            if bias is not None:
+                value = value + vec[pl.ds(bias, 1), pl.ds(low, 256)]
+            projected[:, pl.ds(here, 256)] = to_half(value)
+    allowed = allowed_block(lengths)
+    for pair in range(HEADS // 2):
+        lanes = pair * PAIR
+        queries = halves(projected[:, pl.ds(lanes, PAIR)])
+        keys = projected[:, pl.ds(D + lanes, PAIR)]
+        values = halves(projected[:, pl.ds(2 * D + lanes, PAIR)])
+        total = jnp.zeros((ROWS, PAIR), jnp.float32)
+        for side in (0, 1):
+            scores = jnp.where(allowed, nt(queries[side], keys) * SCALE, MASKED)
+            powers = jnp.exp(scores - jnp.max(scores, -1, keepdims=True))
+            weights = powers * (1.0 / jnp.sum(powers, -1, keepdims=True))
+            weighting[2 * pair + side] = weights
+            total = total + nn(to_half(weights), values[side])
+        rights[1, :, pl.ds(lanes, PAIR)] = to_half(total)
+    first_sum = hidden[...] + nt(rights[1], wide[pl.ds(3 * D, D), :]) + row(O_B)
+    hat, inverse = norm_forward(first_sum)
+    hat_one[...] = hat
+    inverse_one[...] = inverse
+    middle = hat * row(LN1_G) + row(LN1_B)
+    half = to_half(middle)
+    rights[2] = half
+    total = middle + row(FFO_B)
+    for low in range(0, FF, CHUNK):
+        inner = nt(half, wide[pl.ds(4 * D + low, CHUNK), :]) + ff_b[:, pl.ds(low, CHUNK)]
+        square = inner * inner
+        bend = jnp.tanh(GELU_A * inner * (1.0 + GELU_B * square))
+        act = to_half(0.5 * inner * (1.0 + bend))
+        slope[:, pl.ds(low, CHUNK)] = 0.5 * (1.0 + bend) + (0.5 * GELU_A) * inner * (
+            1.0 - bend * bend
+        ) * (1.0 + 3.0 * GELU_B * square)
+        active[pl.ds(low, CHUNK), :] = act.T
+        total = total + nn(act, tall[pl.ds(low, CHUNK), :])
+    hat, inverse = norm_forward(total)
+    hat_two[...] = hat
+    inverse_two[...] = inverse
+    output = hat * row(LN2_G) + row(LN2_B)
+    hidden[...] = output
+    final[...] = output
+
+
+def whole_spec():
+    return pl.BlockSpec(memory_space=VMEM_SPACE, pipeline_mode=pl.Buffered(1))
+
+
+def by_layer(*shape, order=lambda i: i):
+    return pl.BlockSpec(
+        (None, *shape), lambda i: (order(i),) + (0,) * len(shape), memory_space=VMEM_SPACE
+    )
+
+
+def run_forward(lengths, start, wide, tall, vec, ff_b):
+    def kept(*shape, dtype=jnp.bfloat16):
+        return jax.ShapeDtypeStruct((LAYERS, *shape), dtype)
+
+    single = jnp.float32
+    names = (
+        "final",
+        "rights",
+        "projected",
+        "weighting",
+        "hat_one",
+        "inverse_one",
+        "slope",
+        "active",
+        "hat_two",
+        "inverse_two",
+    )
+    outs = pl.pallas_call(
+        forward_kernel,
+        grid=(LAYERS,),
+        out_shape=[
+            jax.ShapeDtypeStruct((ROWS, D), single),
+            jax.ShapeDtypeStruct((3, LAYERS, ROWS, D), jnp.bfloat16),
+            kept(ROWS, 3 * D),
+            kept(HEADS, ROWS, ROWS, dtype=single),
+            kept(ROWS, D, dtype=single),
+            kept(ROWS, 1, dtype=single),
+            kept(ROWS, FF, dtype=single),
+            jax.ShapeDtypeStruct((FF, LAYERS * ROWS), jnp.bfloat16),
+            kept(ROWS, D, dtype=single),
+            kept(ROWS, 1, dtype=single),
+        ],
+        in_specs=[pl.BlockSpec(memory_space=pltpu.SMEM)] + [whole_spec()] * 5,
+        out_specs=[
+            pl.BlockSpec((ROWS, D), lambda i: (0, 0)),
+            pl.BlockSpec((3, None, ROWS, D), lambda i: (0, i, 0, 0)),
+            by_layer(ROWS, 3 * D),
+            by_layer(HEADS, ROWS, ROWS),
+            by_layer(ROWS, D),
+            by_layer(ROWS, 1),
+            by_layer(ROWS, FF),
+            pl.BlockSpec((FF, ROWS), lambda i: (0, i)),
+            by_layer(ROWS, D),
+            by_layer(ROWS, 1),
+        ],
+        scratch_shapes=[VMEM_SPACE((ROWS, D), single)],
+        compiler_params=pltpu.CompilerParams(
+            dimension_semantics=("arbitrary",), vmem_limit_bytes=VMEM_ASK
+        ),
+    )(lengths, start, wide, tall, vec, ff_b)
+    return dict(zip(names, outs))
+
+
+def backward_kernel(
+    start,
+    wide,
+    tall,
+    vec,
+    projected,
+    weighting,
+    hat_one,
+    inverse_one,
+    slope,
+    hat_two,
+    inverse_two,
+    result,
+    turned,
+    outer,
+    sums,
+    ff_sum,
+    upstream,
+    back_mixed,
+    joint,
+):
+    step = pl.program_id(0)
+
+    @pl.when(step == 0)
+    def _():
+        upstream[...] = start[...]
+        sums[...] = jnp.zeros_like(sums)
+        ff_sum[...] = jnp.zeros_like(ff_sum)
+
+    def row(index):
+        return vec[pl.ds(index, 1), :]
+
+    def add_sum(index, value):
+        here = pl.ds(index - Q_B, 1)
+        sums[here, :] = sums[here, :] + jnp.sum(value, 0, keepdims=True)
+
+    up = upstream[...]
+    hat = hat_two[...]
+    add_sum(LN2_G, up * hat)
+    add_sum(LN2_B, up)
+    back_second = norm_backward(up, row(LN2_G), hat, inverse_two[...])
+    half = to_half(back_second)
+    outer[...] = half
+    add_sum(FFO_B, half.astype(jnp.float32))
+    total = back_second
+    for low in range(0, FF, CHUNK):
+        lanes = pl.ds(low, CHUNK)
+        inner = to_half(nt(half, tall[lanes, :]) * slope[:, lanes])
+        ff_sum[:, lanes] = ff_sum[:, lanes] + jnp.sum(
+            inner.astype(jnp.float32), 0, keepdims=True
+        )
+        turned[pl.ds(4 * D + low, CHUNK), :] = inner.T
+        total = total + nn(inner, wide[pl.ds(4 * D + low, CHUNK), :])
+    hat = hat_one[...]
+    add_sum(LN1_G, total * hat)
+    add_sum(LN1_B, total)
+    back_first = norm_backward(total, row(LN1_G), hat, inverse_one[...])
+    upstream[...] = back_first
+    half = to_half(back_first)
+    add_sum(O_B, half.astype(jnp.float32))
+    turned[pl.ds(3 * D, D), :] = half.T
+    back_mixed[...] = to_half(nn(half, wide[pl.ds(3 * D, D), :]))
+    for pair in range(HEADS // 2):
+        lanes = pair * PAIR
+        queries = halves(projected[:, pl.ds(lanes, PAIR)])
+        keys = halves(projected[:, pl.ds(D + lanes, PAIR)])
+        values = projected[:, pl.ds(2 * D + lanes, PAIR)]
+        grads = halves(back_mixed[:, pl.ds(lanes, PAIR)])
+        zero = jnp.zeros((ROWS, PAIR), jnp.float32)
+        back_query, back_key, back_value = zero, zero, zero
+        for side in (0, 1):
+            weights = weighting[2 * pair + side]
+            soft = nt(grads[side], values)
+            scores = to_half(
+                weights * (soft - jnp.sum(weights * soft, -1, keepdims=True))
+            )
+            back_query = back_query + nn(scores, keys[side])
+            back_key = back_key + tn(scores, queries[side])
+            back_value = back_value + tn(to_half(weights), grads[side])
+        joint[:, pl.ds(lanes, PAIR)] = to_half(back_query * SCALE)
+        joint[:, pl.ds(D + lanes, PAIR)] = to_half(back_key * SCALE)
+        joint[:, pl.ds(2 * D + lanes, PAIR)] = to_half(back_value)
+    total = upstream[...]
+    for part, bias in ((0, Q_B), (1, None), (2, V_B)):
+        here = pl.ds(part * D, D)
+        value = joint[:, here]
+        if bias is not None:
+            add_sum(bias, value.astype(jnp.float32))
+        turned[here, :] = value.T
+        total = total + nn(value, wide[here, :])
+    upstream[...] = total
+    result[...] = total
+
+
+def run_backward(start, wide, tall, vec, kept):
+    single, half = jnp.float32, jnp.bfloat16
+    last = LAYERS - 1
+
+    def order(i):
+        return last - i
+
+    return pl.pallas_call(
+        backward_kernel,
+        grid=(LAYERS,),
+        out_shape=[
+            jax.ShapeDtypeStruct((ROWS, D), single),
+            jax.ShapeDtypeStruct((4 * D + FF, LAYERS * ROWS), half),
+            jax.ShapeDtypeStruct((LAYERS, ROWS, D), half),
+            jax.ShapeDtypeStruct((8, D), single),
+            jax.ShapeDtypeStruct((1, FF), single),
+        ],
+        in_specs=[whole_spec()] * 4
+        + [
+            by_layer(ROWS, 3 * D, order=order),
+            by_layer(HEADS, ROWS, ROWS, order=order),
+            by_layer(ROWS, D, order=order),
+            by_layer(ROWS, 1, order=order),
+            by_layer(ROWS, FF, order=order),
+            by_layer(ROWS, D, order=order),
+            by_layer(ROWS, 1, order=order),
+        ],
+        out_specs=[
+            pl.BlockSpec((ROWS, D), lambda i: (0, 0)),
+            pl.BlockSpec((4 * D + FF, ROWS), lambda i: (0, order(i))),
+            by_layer(ROWS, D, order=order),
+            pl.BlockSpec((8, D), lambda i: (0, 0)),
+            pl.BlockSpec((1, FF), lambda i: (0, 0)),
+        ],
+        scratch_shapes=[
+            VMEM_SPACE((ROWS, D), single),
+            VMEM_SPACE((ROWS, D), half),
+            VMEM_SPACE((ROWS, 3 * D), half),
+        ],
+        compiler_params=pltpu.CompilerParams(
+            dimension_semantics=("arbitrary",), vmem_limit_bytes=VMEM_ASK
+        ),
+    )(
+        start,
+        wide,
+        tall,
+        vec,
+        kept["projected"],
+        kept["weighting"],
+        kept["hat_one"],
+        kept["inverse_one"],
+        kept["slope"],
+        kept["hat_two"],
+        kept["inverse_two"],
+    )
 
 
 def adam_update(weight, gradient, first, second, rate):
@@ -933,7 +1636,7 @@
     words = word_table.shape[0]
     slots = mlm_labels.shape[0]
     pieces = split_vectors(vectors)
-    token_kind, allowed = row_layout(seq_lengths)
+    token_kind = row_kind(seq_lengths)
 
     facts = jnp.concatenate([token_ids, mlm_labels, seq_lengths])
     padded = -(-facts.shape[0] // 1024) * 1024
@@ -973,12 +1676,9 @@
     normed_half = to_half(embed_hat * pieces["emb_g"] + pieces["emb_b"])
     hidden = product(normed_half, head[E + D :]) + pieces["proj_b"]
 
-    final, kept = lax.scan(
-        lambda h, unused: layer_forward(h, wide, tall, pieces, allowed),
-        hidden,
-        None,
-        length=LAYERS,
-    )
+    vec = vectors[: 10 * D].reshape(10, D)
+    kept = run_forward(seq_lengths, hidden, wide, tall, vec, pieces["ff_b"][None])
+    final = kept["final"]
 
     final_half = to_half(final)
     pick = to_half(mlm_rows[:, None] == jnp.arange(ROWS, dtype=jnp.int32)[None, :])
@@ -1052,61 +1752,24 @@
         + jnp.where(row_index == BUCKET, back_firsts[1:2], 0.0)
     )
 
-    back_hidden, back = lax.scan(
-        lambda up, k: layer_backward(up, k, wide, tall, pieces), back_final, kept, reverse=True
+    back_hidden, turned, outer, layer_sums, ff_sum = run_backward(
+        back_final, wide, tall, vec, kept
     )
 
     upstream_half = to_half(back_hidden)
     back_normed = times_transpose(upstream_half, head[E + D :])
     back_proj = transpose_times(normed_half, upstream_half)
     back_embedded = norm_backward(back_normed, pieces["emb_g"], embed_hat, embed_inverse)
-    (all_back,) = network.gather([to_half(back_embedded)])
-    back_word = back_word_head + transpose_times(select, all_back)
-    places = position_table.shape[0]
-    by_device = all_back.reshape(devices, ROWS, E)
-    folded = by_device[:, :BUCKET].astype(jnp.float32) + jnp.where(
-        all_seconds[:, None, None], by_device[:, BUCKET:].astype(jnp.float32), 0.0
-    )
-    rest = jnp.where(all_seconds[:, None, None], 0.0, by_device[:, BUCKET:].astype(jnp.float32))
-    all_place = jnp.concatenate([jnp.sum(folded, 0), jnp.sum(rest, 0)], 0)
-    all_place = jnp.pad(all_place, ((0, places * devices - ROWS), (0, 0)))
-    back_place = lax.dynamic_slice(all_place, (own * places, 0), (places, E))
-
-    def long(x):
-        return x.reshape(-1, x.shape[-1])
-
-    joint_all, branch_all = long(back["joint_half"]), long(back["branch_half"])
-    inner_all, outer_all = long(back["inner_half"]), long(back["outer_half"])
-    back_wide = jnp.concatenate(
-        [
-            to_half(transpose_times(joint_all, long(kept["hidden_half"]))),
-            to_half(transpose_times(branch_all, long(kept["mixed"]))),
-            to_half(transpose_times(inner_all, long(kept["middle_half"]))),
-        ],
-        0,
-    )
-    back_tall = to_half(transpose_times(long(kept["active"]), outer_all))
-    back_head = to_half(jnp.concatenate([back_mlm, back_pool, back_proj], 0))
-    sum_wide, sum_tall, sum_head = network.scatter([back_wide, back_tall, back_head])
-
-    joint_sum = column_sum(joint_all)
-    norms = jnp.sum(back["norms"], 0)
+    back_head = jnp.concatenate([back_mlm, back_pool, back_proj], 0)
     kind_one = jnp.sum(jnp.where(token_kind[:, None] == 1, back_embedded, 0.0), 0)
     kind_zero = jnp.sum(jnp.where(token_kind[:, None] == 0, back_embedded, 0.0), 0)
     vector_grad = join_vectors(
         {
             "proj_b": column_sum(upstream_half),
-            "q_b": joint_sum[:D],
-            "v_b": joint_sum[2 * D :],
-            "o_b": column_sum(branch_all),
-            "ln1_g": norms[0],
-            "ln1_b": norms[1],
-            "ffo_b": column_sum(outer_all),
-            "ln2_g": norms[2],
-            "ln2_b": norms[3],
+            "layer": layer_sums,
             "pool_b": column_sum(pre_half),
             "cls": back_cls,
-            "ff_b": column_sum(inner_all),
+            "ff_b": ff_sum,
             "emb_g": jnp.sum(back_normed * embed_hat, 0),
             "emb_b": jnp.sum(back_normed, 0),
             "mlm_b": column_sum(dense_half),
@@ -1115,13 +1778,29 @@
             "types": jnp.concatenate([kind_zero, kind_one]),
         }
     )
+    sum_wide, sum_tall, sum_head, all_back, own_vector = network.finish(
+        turned,
+        kept["active"],
+        kept["rights"].reshape(3, -1, D),
+        outer.reshape(-1, D),
+        back_head,
+        to_half(back_embedded),
+        vector_grad,
+    )
+    back_word = back_word_head + transpose_times(select, all_back)
+    places = position_table.shape[0]
+    by_device = all_back.reshape(devices, ROWS, E)
+    folded = by_device[:, :BUCKET].astype(jnp.float32) + jnp.where(
+        all_seconds[:, None, None], by_device[:, BUCKET:].astype(jnp.float32), 0.0
+    )
+    rest = jnp.where(all_seconds[:, None, None], 0.0, by_device[:, BUCKET:].astype(jnp.float32))
+    all_place = jnp.concatenate([jnp.sum(folded, 0), jnp.sum(rest, 0)], 0)
+    all_place = jnp.pad(all_place, ((0, places * devices - ROWS), (0, 0)))
+    back_place = lax.dynamic_slice(all_place, (own * places, 0), (places, E))
     shards = (back_word, back_place, sum_head.T, back_decoder, sum_wide.T, sum_tall)
     local_squares = jnp.sum(jnp.stack([jnp.sum(s * s) for s in shards]))
     total = vector_grad.shape[0]
     share = -(-total // (devices * 1024)) * 1024
-    own_vector = network.scatter_small(
-        jnp.pad(vector_grad, (0, devices * share - total)).reshape(devices, -1, 128)
-    )
     scalars = jnp.stack([sop_sum, local_squares])
     scalars = jnp.pad(scalars, (0, 1024 - scalars.shape[0])).reshape(8, 128)
     (last,) = network.gather_small([jnp.concatenate([own_vector, scalars], 0)])

time: 664 us -> 476 us (0.72)
  matrix products: 175 us -> 32.9 us
  Pallas kernels: 269 us -> 358 us
  other arithmetic: 129 us -> 45.7 us
  local copies, waits for them, and re-layouts: 70.4 us -> 19.9 us
    pallas_call x0 -> x3, Pallas kernels: none -> 197 us  [the longest x1 106 us: run_finish(): pl.pallas_call(functools.partial(finish_kernel, planes, heights, split),...]
    pallas_call x2 -> x1, Pallas kernels: 97.4 us -> 26.2 us  [big_scatter(): pl.pallas_call(functools.partial(big_scatter_kernel, planes, rows, tuple(...]
    dot_general x20 -> x4, matrix products: 67.2 us -> 4.59 us  [times_transpose(): lax.dot_general(a, b, (((1,), (1,)), ((), ())), preferred_element_type=jn...]
    dot_general x22 -> x6, matrix products: 49 us -> 13.8 us  [product(): return jnp.dot(a, b, preferred_element_type=jnp.float32)]
    dynamic_update_slice x24 -> x0, other arithmetic: 30.3 us -> none  [the longest x20 27.8 us: local(): lax.scan(lambda h, unused: layer_forward(h, wide, tall, pieces, allowed),...]
    dot_general x24 -> x0, matrix products: 28.1 us -> none  [the longest x4 10.1 us: layer_backward(): jnp.einsum('qhd,khd->hqk', back_mixed, values, preferred_element_type=jnp...]
    pallas_call x2 -> x1, Pallas kernels: 92.2 us -> 70.2 us  [big_gather(): pl.pallas_call(functools.partial(big_gather_kernel, planes, rows, tuple(m...]
    concatenate x6 -> x1, other arithmetic: 23.1 us -> 1.24 us  [local(): back_head = jnp.concatenate([back_mlm, back_pool, back_proj], 0)]
where the time goes in v3:
time: 476 us; the launch traced here: 469 us
  Pallas kernels  358 us (75%)
  other arithmetic  45.7 us (10%)
  matrix products  32.9 us (7%)
  local copies, waits for them, and re-layouts  19.9 us (4%)
  between operations  11.8 us (2%)
    pallas_call x1, Pallas kernels, run_finish(): pl.pallas_call(functools.partial(finish_kernel, planes, heights, split),...  106 us
    pallas_call x1, Pallas kernels, big_gather(): pl.pallas_call(functools.partial(big_gather_kernel, planes, rows, tuple(m...  70.2 us
    pallas_call x4, Pallas kernels, small_gather(): pl.pallas_call(functools.partial(small_gather_kernel, count, planes, widt...  48.3 us
    pallas_call x1, Pallas kernels, run_forward(): pl.pallas_call(forward_kernel, grid=(LAYERS,), out_shape=[jax.ShapeDtypeS...  45.9 us
    pallas_call x1, Pallas kernels, run_backward(): pl.pallas_call(backward_kernel, grid=(LAYERS,), out_shape=[jax.ShapeDtype...  45.4 us
    pallas_call x1, Pallas kernels, big_scatter(): pl.pallas_call(functools.partial(big_scatter_kernel, planes, rows, tuple(...  26.2 us
    pallas_call x1, Pallas kernels, small_scatter(): pl.pallas_call(functools.partial(small_scatter_kernel, planes, width), ou...  16.1 us
    dot_general x6, matrix products, product(): return jnp.dot(a, b, preferred_element_type=jnp.float32)  13.8 us

profile of v3, /device:TPU:0, one launch (start us, length us, event | category | flops | bytes accessed | tf_op | source)
XLA Modules:
  0.0 468.5 jit_solution(8689866568151617532)
XLA Ops:
  7.5 70.2 %shard_map.451 = (bf16[4,4,2,192,768]{4,3,2,1,0:T(8,128)(2,1)}, bf16[4,4,2,96,768]{4,3,2,1,0:T(8,128)(2,1)}, bf16[4,4,2,32,768]{4,3,2,1,0:T(8,128)(2,1)}) custom-call(bf16[320,768]{1,0:T(8,128)(2,1)} %pad_maximum_fusion.1.x), custom_call_target="tpu_custom_call" | custom-call | tf_op jit(solution)/shard_map/pallas_call | solution.py:467
  79.0 1.8 broadcast_compare_fusion
  82.1 12.3 %shard_map.449 = (s32[4,8,8,128]{3,2,1,0:T(8,128)}, f32[4,8,16,128]{3,2,1,0:T(8,128)}) custom-call(s32[8,128]{1,0:T(8,128)} %pad_bitcast_fusion.refs_0_, f32[16,128]{1,0:T(8,128)} %convert_convert_fusion.refs_1_), custom_call_target="tpu_custom_call" | custom-call | tf_op jit(solution)/shard_map/pallas_call | solution.py:215
  95.5 10.1 %fusion.4 = bf16[8192,128]{1,0:T(8,128)(2,1)} fusion(s32[8192]{0:T(1024)S(1)} %bitcast.121, f32[960,128]{1,0:T(8,128)S(1)} %copy-done.2), kind=kOutput, calls=%fused_computation.5 | convolution fusion | flops 2022301696 | bytes 2621440 | tf_op jit(solution)/shard_map/dot_general | solution.py:78
  105.6 26.2 %shard_map.450 = f32[256,128]{1,0:T(8,128)} custom-call(bf16[4,4,2,256,128]{4,3,2,1,0:T(8,128)(2,1)} %bitcast.108), custom_call_target="tpu_custom_call" | custom-call | tf_op jit(solution)/shard_map/pallas_call | solution.py:731
  135.7 45.9 %shard_map.452 = (f32[256,768]{1,0:T(8,128)}, bf16[3,4,256,768]{3,2,1,0:T(8,128)(2,1)}, bf16[4,256,2304]{2,1,0:T(8,128)(2,1)}, f32[4,12,256,256]{3,2,1,0:T(8,128...) custom-call(s32[2]{0:T(128)} %lengths.1, ...), custom_call_target="tpu_custom_call" | custom-call | tf_op jit(solution)/shard_map/pallas_call | solution.py:1407
  185.0 11.0 %shard_map.453 = bf16[4,8,48,128]{3,2,1,0:T(8,128)(2,1)} custom-call(bf16[48,128]{1,0:T(8,128)(2,1)} %pad.25.refs_0_), custom_call_target="tpu_custom_call" | custom-call | tf_op jit(solution)/shard_map/pallas_call | solution.py:215
  197.0 3.1 fusion.76
  200.1 3.7 exponential_reduce_fusion
  204.5 13.9 %shard_map.454 = f32[4,8,32,128]{3,2,1,0:T(8,128)} custom-call(f32[32,128]{1,0:T(8,128)} %fusion.42.refs_0_), custom_call_target="tpu_custom_call" | custom-call | tf_op jit(solution)/shard_map/pallas_call | solution.py:215
  218.4 1.3 copy.78
  223.8 4.0 convert_reduce_fusion
  228.7 1.8 fusion.53
  230.5 16.1 %shard_map.455 = f32[40,128]{1,0:T(8,128)} custom-call(f32[4,8,40,128]{3,2,1,0:T(8,128)} %bitcast.103), custom_call_target="tpu_custom_call" | custom-call | tf_op jit(solution)/shard_map/pallas_call | solution.py:269
  255.6 1.6 fusion.8.start
  257.2 45.4 %shard_map.456 = (f32[256,768]{1,0:T(8,128)}, bf16[6144,1024]{1,0:T(8,128)(2,1)}, bf16[4,256,768]{2,1,0:T(8,128)(2,1)}, f32[8,768]{1,0:T(8,128)}, f32[1,3072]{1,0:T(1,128)}) custom-call(f32[256,768]{1,0:T(8,128)} %fusion.8.start, bf16[6144,768]{1,0:T(8,128)(2,1)} %bitcast.92, bf16[3072,768]{1,0:T(8,128)(2,1)} %bitcast.94, f32[10,768]{1,0:T(8,128)} %reshape.357.vec, ...), custom_call_target="tpu_custom_call" | custom-call | tf_op jit(solution)/shard_map/pallas_call | solution.py:1544
  302.7 1.5 convolution_convert_fusion.1
  315.7 106.2 %shard_map.457 = (f32[320,768]{1,0:T(8,128)}, bf16[4,4,2,256,128]{4,3,2,1,0:T(8,128)(2,1)}, f32[8,128]{1,0:T(8,128)}) custom-call(bf16[6144,1024]{1,0:T(8,128)(2,1)} %get-tuple-element.62.left_wide, bf16[3072,1024]{1,0:T(8,128)(2,1)} %get-tuple-element.63.left_tall, bf16[3,1024,768]{2,1,0:T(8,128)(2,1)} %bitcast.102, bf16[1024,768]{1,0:T(8,128)(2,1)} %bitcast.110, ...), custom_call_target="tpu_custom_call" | custom-call | tf_op jit(solution)/shard_map/pallas_call | solution.py:1139
  422.0 8.4 %multiply_reduce_fusion.1 = (f32[]{:T(128)}, f32[960,128]{1,0:T(8,128)}) fusion(f32[960,128]{1,0:T(8,128)S(1)} %fusion.77, bf16[8192,128]{1,0:T(8,128)(2,1)} %bitcast.106, s32[8192]{0:T(1024)S(1)} %bitcast.122), kind=kOutput, calls=%fused_computation.45 | convolution fusion | flops 2021498880 | bytes 3112964 | tf_op jit(solution)/shard_map/dot_general | solution.py:86
  430.4 2.2 fusion.7
  442.0 11.1 %shard_map.458 = f32[4,8,16,128]{3,2,1,0:T(8,128)} custom-call(f32[16,128]{1,0:T(8,128)} %pad_maximum_fusion.2.refs_0_), custom_call_target="tpu_custom_call" | custom-call | tf_op jit(solution)/shard_map/pallas_call | solution.py:215
  453.1 1.7 slice_reduce_fusion.1
  457.8 2.7 multiply_subtract_fusion.1
  462.6 1.5 multiply_subtract_fusion
  (236 shorter events, 53.0 us)
Async XLA Ops:
  0.7 94.8 %copy-start.2 = (f32[960,128]{1,0:T(8,128)S(1)}, f32[960,128]{1,0:T(8,128)}, u32[]{:S(2)}) copy-start(f32[960,128]{1,0:T(8,128)} %param.26) | copy-start | bytes 1474564
  0.7 77.1 %copy-start.39 = (s32[2]{0:T(128)S(1)}, s32[2]{0:T(128)}, u32[]{:S(2)}) copy-start(s32[2]{0:T(128)} %lengths.1) | copy-start | bytes 28
  0.7 80.2 %copy-start.61 = (s32[40]{0:T(128)S(1)}, s32[40]{0:T(128)}, u32[]{:S(2)}) copy-start(s32[40]{0:T(128)} %param.50) | copy-start | bytes 484
  0.7 80.2 %copy-start.60 = (s32[256]{0:T(256)S(1)}, s32[256]{0:T(256)}, u32[]{:S(2)}) copy-start(s32[256]{0:T(256)} %param.47) | copy-start | bytes 3076
  0.7 80.8 %copy-start.23 = (f32[16,128]{1,0:T(8,128)S(1)}, f32[16,128]{1,0:T(8,128)}, u32[]{:S(2)}) copy-start(f32[16,128]{1,0:T(8,128)} %param.27) | copy-start | bytes 24580
  2.4 130.8 %copy-start.33 = (f32[128]{0:T(128)}, f32[128]{0:T(128)S(1)}, u32[]{:S(2)}) copy-start(f32[128]{0:T(128)S(1)} %get-tuple-element.143) | copy-start | bytes 1540
  2.4 130.8 %copy-start.44 = (f32[128]{0:T(128)}, f32[128]{0:T(128)S(1)}, u32[]{:S(2)}) copy-start(f32[128]{0:T(128)S(1)} %get-tuple-element.142) | copy-start | bytes 1540
  2.4 181.9 %copy-start.35 = (f32[128]{0:T(128)}, f32[128]{0:T(128)S(1)}, u32[]{:S(2)}) copy-start(f32[128]{0:T(128)S(1)} %get-tuple-element.141) | copy-start | bytes 1540
  80.8 51.0 %copy-start.48 = (pred[256]{0:T(512)(128)(4,1)}, pred[256]{0:T(512)(128)(4,1)S(1)}, u32[]{:S(2)}) copy-start(pred[256]{0:T(512)(128)(4,1)S(1)} %get-tuple-element.156) | copy-start | bytes 772
  95.4 127.0 %copy-start.10 = (s32[4,8,8,128]{3,1,2,0:T(8,128)}, s32[4,8,8,128]{3,1,2,0:T(8,128)S(1)}, u32[]{:S(2)}) copy-start(s32[4,8,8,128]{3,1,2,0:T(8,128)S(1)} %copy.79) | copy-start | bytes 393220
  95.5 36.4 %copy-start.20 = (f32[4,8,16,128]{3,2,1,0:T(8,128)S(1)}, f32[4,8,16,128]{3,2,1,0:T(8,128)}, u32[]{:S(2)}) copy-start(f32[4,8,16,128]{3,2,1,0:T(8,128)} %get-tuple-element.50) | copy-start | bytes 786436
  105.6 27.6 %copy-start.1 = (bf16[4,4,2,32,768]{4,3,2,1,0:T(8,128)(2,1)S(1)}, bf16[4,4,2,32,768]{4,3,2,1,0:T(8,128)(2,1)}, u32[]{:S(2)}) copy-start(bf16[4,4,2,32,768]{4,3,2,1,0:T(8,128)(2,1)} %get-tuple-element.51) | copy-start | bytes 4718596
  105.6 28.9 %slice-start = ((f32[13184]{0:T(1024)}), f32[7680]{0:T(1024)S(1)}, s32[]{:S(2)}) async-start(f32[13184]{0:T(1024)} %param.32), calls=%async_computation | async-start | bytes 65536 | tf_op jit(solution)/shard_map/slice | solution.py:1679
  105.6 29.5 %copy-start.13 = (f32[13184]{0:T(1024)S(1)}, f32[13184]{0:T(1024)}, u32[]{:S(2)}) copy-start(f32[13184]{0:T(1024)} %param.32) | copy-start | bytes 158212
  133.2 48.4 %copy-start.28 = (f32[256]{0:T(256)}, f32[256]{0:T(256)S(1)}, u32[]{:S(2)}) copy-start(f32[256]{0:T(256)S(1)} %add_rsqrt_fusion) | copy-start | bytes 3076
  135.7 47.8 %copy-start.62 = (s32[40]{0:T(128)S(1)}, s32[40]{0:T(128)}, u32[]{:S(2)}) copy-start(s32[40]{0:T(128)} %param.49) | copy-start | bytes 484
  249.3 53.3 %copy-start.19 = (bf16[40,128]{1,0:T(8,128)(2,1)}, bf16[40,128]{1,0:T(8,128)(2,1)S(1)}, u32[]{:S(2)}) copy-start(bf16[40,128]{1,0:T(8,128)(2,1)S(1)} %get-tuple-element.125) | copy-start | bytes 30724
  250.3 52.3 %copy-start.27 = (bf16[1,768]{1,0:T(2,128)(2,1)}, bf16[1,768]{1,0:T(2,128)(2,1)S(1)}, u32[]{:S(2)}) copy-start(bf16[1,768]{1,0:T(2,128)(2,1)S(1)} %get-tuple-element.134) | copy-start | bytes 4612
  253.9 48.7 %copy-start.50 = (f32[2]{0:T(128)}, f32[2]{0:T(128)S(1)}, u32[]{:S(2)}) copy-start(f32[2]{0:T(128)S(1)} %get-tuple-element.95) | copy-start | bytes 28
  257.2 45.4 %copy-start.29 = (f32[256]{0:T(256)S(1)}, f32[256]{0:T(256)}, u32[]{:S(2)}) copy-start(f32[256]{0:T(256)} %copy-done.28) | copy-start | bytes 3076
  257.2 45.4 %copy-start.34 = (f32[128]{0:T(128)S(1)}, f32[128]{0:T(128)}, u32[]{:S(2)}) copy-start(f32[128]{0:T(128)} %copy-done.33) | copy-start | bytes 1540
  257.2 45.4 %copy-start.45 = (f32[128]{0:T(128)S(1)}, f32[128]{0:T(128)}, u32[]{:S(2)}) copy-start(f32[128]{0:T(128)} %copy-done.44) | copy-start | bytes 1540
  257.2 48.2 %copy-start.16 = (bf16[40,768]{1,0:T(8,128)(2,1)S(1)}, bf16[40,768]{1,0:T(8,128)(2,1)}, u32[]{:S(2)}) copy-start(bf16[40,768]{1,0:T(8,128)(2,1)} %copy-done.15) | copy-start | bytes 184324
  315.7 106.3 %copy-start.26 = (s32[4,2,8,128]{3,1,2,0:T(2,128)S(1)}, s32[4,2,8,128]{3,1,2,0:T(2,128)}, u32[]{:S(2)}) copy-start(s32[4,2,8,128]{3,1,2,0:T(2,128)} %copy-done.25) | copy-start | bytes 98308
  (41 other events, 468.6 us)
